TPU v7x, 128 devices: a whole 4x4x4 slice. The times are simulated.
128 devices in a mesh: row: 16 (over x_lo, z, core), col: 8 (over y, x_hi).
Axes of the slice: x: 4 (x_hi: 2, x_lo: 2; x = x_hi * 2 + x_lo), y: 4, z: 4, core: 2. Of those that a mesh axis runs over, the one named last changes fastest.
Arguments:
- tokens: bfloat16 [256, 8192], P('col', 'row'), may hold values from -6 to 6
- out_grad: bfloat16 [256, 8192], P('col', 'row'), may hold values from -0.75 to 0.75
- token_weight: float32 [256], replicated, may hold values from -0.4375 to 0.4375
- gate_weight: bfloat16 [8192, 29568], P('row', 'col'), may hold values from -0.0625 to 0.0625
- up_weight: bfloat16 [8192, 29568], P('row', 'col'), may hold values from -0.0625 to 0.0625
- down_weight: bfloat16 [29568, 8192], P('col', 'row'), may hold values from -0.03125 to 0.03125
Outputs:
- input_grad: float32 [256, 8192], P('col', 'row')
- gate_grad: bfloat16 [8192, 29568], P('row', 'col')
- up_grad: bfloat16 [8192, 29568], P('row', 'col')
- down_grad: bfloat16 [29568, 8192], P('col', 'row')
All inputs are finite; a program needn't handle non-finite values.
Results may differ from a plain program's by a relative error of at most 0.0049.
Values may be sent and summed in bfloat16 or wider, within the bound.
A program may use at most 128 MiB of HBM per device.

v0:
```python
import jax
import jax.numpy as jnp
from jax import lax
from jax.sharding import PartitionSpec as P


def swiglu_back(summed, weights, width):
    gate = summed[:, :width]
    up = summed[:, width : 2 * width]
    back = summed[:, 2 * width :]
    column = weights[:, None]
    sig = jax.nn.sigmoid(gate)
    silu = gate * sig
    weighted_hidden = (column * (silu * up)).astype(jnp.bfloat16)
    scaled = column * back
    gate_back = (scaled * up * sig * (1.0 + gate * (1.0 - sig))).astype(jnp.bfloat16)
    up_back = (scaled * silu).astype(jnp.bfloat16)
    return (weighted_hidden, gate_back, up_back)


def body(tokens, out_grad, token_weight, gate_weight, up_weight, down_weight):
    acts, grads = (
        lax.all_gather(tokens, "col", axis=0, tiled=True),
        lax.all_gather(out_grad, "col", axis=0, tiled=True),
    )
    total = acts.shape[0]
    width = gate_weight.shape[1]
    over_tokens = (((0,), (0,)), ((), ()))
    over_hidden = (((1,), (1,)), ((), ()))
    share = total // lax.axis_size("row")
    rows_x = acts
    rows_d = grads
    gate_part = jnp.dot(rows_x, gate_weight, preferred_element_type=jnp.float32)
    up_part = jnp.dot(rows_x, up_weight, preferred_element_type=jnp.float32)
    back_part = lax.dot_general(
        rows_d, down_weight, over_hidden, preferred_element_type=jnp.float32
    )
    summed = lax.psum_scatter(
        jnp.concatenate([gate_part, up_part, back_part], axis=1),
        "row",
        scatter_dimension=0,
        tiled=True,
    )
    first = lax.axis_index("row") * share
    weights = lax.dynamic_slice_in_dim(token_weight, first, share, 0)
    weighted_hidden, gate_back, up_back = swiglu_back(summed, weights, width)
    hidden_piece = lax.all_gather(weighted_hidden, "row", axis=0, tiled=True)
    gate_piece = lax.all_gather(gate_back, "row", axis=0, tiled=True)
    up_piece = lax.all_gather(up_back, "row", axis=0, tiled=True)
    rows_x = acts
    rows_d = grads
    gate_acc = lax.dot_general(rows_x, gate_piece, over_tokens, preferred_element_type=jnp.float32)
    up_acc = lax.dot_general(rows_x, up_piece, over_tokens, preferred_element_type=jnp.float32)
    down_acc = lax.dot_general(
        hidden_piece, rows_d, over_tokens, preferred_element_type=jnp.float32
    )
    rows_in = lax.dot_general(
        gate_piece, gate_weight, over_hidden, preferred_element_type=jnp.float32
    )
    rows_in = rows_in + lax.dot_general(
        up_piece, up_weight, over_hidden, preferred_element_type=jnp.float32
    )
    input_grad = lax.psum_scatter(rows_in, "col", scatter_dimension=0, tiled=True)
    return (
        input_grad,
        gate_acc.astype(jnp.bfloat16),
        up_acc.astype(jnp.bfloat16),
        down_acc.astype(jnp.bfloat16),
    )


def solution(mesh):
    return jax.shard_map(
        body,
        mesh=mesh,
        in_specs=(
            P("col", "row"),
            P("col", "row"),
            P(),
            P("row", "col"),
            P("row", "col"),
            P("col", "row"),
        ),
        out_specs=(P("col", "row"), P("row", "col"), P("row", "col"), P("col", "row")),
        check_vma=False,
    )
```

profile of v0, /device:TPU:1, one launch (start us, length us, event | category | flops | bytes accessed | tf_op | source)
XLA Modules:
  0.0 375.5 jit_solution(16875857566188045774)
XLA Ops:
  7.2 0.0 reduce-scatter.7.cloned.1.call-start
  7.2 30.5 %all_gather.15 = bf16[256,512]{1,0:T(8,128)(2,1)S(1)} all-gather(bf16[32,512]{1,0:T(8,128)(2,1)} %param.6), channel_id=1, replica_groups=mesh['row'=16,'col'=8] {'col'}, dimensions={0}, use_global_device_ids=true | all-gather | bytes 294912 | tf_op jit(solution)/shard_map/all_gather | solution.py:23
  37.8 0.0 copy-start.3
  37.8 3.4 fusion.3
  41.2 0.0 copy-done.3
  41.2 0.0 copy-start.4
  41.2 0.0 copy-start.2
  41.2 1.2 fusion.4
  42.4 0.0 copy-done.4
  42.4 28.7 %all_gather.16 = bf16[256,512]{1,0:T(8,128)(2,1)S(1)} all-gather(bf16[32,512]{1,0:T(8,128)(2,1)S(1)} %copy-done.4), channel_id=1, replica_groups=mesh['row'=16,'col'=8] {'col'}, dimensions={0}, use_global_device_ids=true | all-gather | bytes 294912 | tf_op jit(solution)/shard_map/all_gather | solution.py:24
  71.1 0.0 copy-done.2
  71.1 1.2 fusion.5
  72.3 10.8 %pad_maximum_fusion = f32[256,11088]{0,1:T(8,128)} fusion(f32[256,3696]{0,1:T(8,128)S(1)} %fusion.5, f32[256,3696]{0,1:T(8,128)S(1)} %fusion.4, f32[256,3696]{0,1:T(8,128)S(1)} %fusion.3), kind=kLoop, calls=%fused_computation | loop fusion | flops 5677056 | bytes 22708224 | tf_op jit(solution)/shard_map/concatenate | solution.py:39
  83.1 11.9 %copy.16 = f32[256,11088]{1,0:T(8,128)} copy(f32[256,11088]{0,1:T(8,128)} %pad_maximum_fusion) | data formatting | bytes 22708224
  95.0 0.0 copy-start.5
  95.0 0.0 reduce-scatter.7.cloned.1.call-update
  95.1 0.0 all-gather.4.cloned.1.call-start
  95.1 0.6 copy-done.5
  95.7 0.1 dynamic_slice.3
  95.8 90.1 %reduce-scatter.7.cloned.1.call-done = f32[16,11088]{1,0:T(8,128)} async-done(((f32[256,11088]{1,0:T(8,128)}), f32[16,11088]{1,0:T(8,128)}) %reduce-scatter.7.cloned.1.call-update) | async-done | bytes 709648 | tf_op jit(solution)/shard_map/reduce_scatter | solution.py:38
  185.9 2.1 multiply_convert_fusion
  188.0 0.0 all-gather.4.cloned.1.call-update
  188.0 0.0 all-gather.6.cloned.1.call-start
  188.1 0.7 all-gather.6.cloned.1.call-update
  188.8 0.0 all-gather.8.cloned.1.call-start
  188.8 0.5 all-gather.8.cloned.1.call-update
  189.4 0.2 reduce-scatter.5.cloned.1.call-start
  189.6 34.8 %all-gather.4.cloned.1.call-done = bf16[256,3696]{1,0:T(8,128)(2,1)} async-done(((bf16[16,3696]{1,0:T(8,128)(2,1)}), bf16[256,3696]{1,0:T(8,128)(2,1)}) %all-gather.4.cloned.1.call-update) | async-done | bytes 1892368 | tf_op jit(solution)/shard_map/all_gather | solution.py:48
  224.4 3.8 %fusion.6 = f32[256,512]{1,0:T(8,128)S(1)} fusion(bf16[256,3696]{1,0:T(8,128)(2,1)} %all-gather.4.cloned.1.call-done, bf16[512,3696]{0,1:T(8,128)(2,1)} %param.9), kind=kOutput, calls=%fused_computation.16 | convolution fusion | flops 968884224 | bytes 6201344 | tf_op jit(solution)/shard_map/dot_general | solution.py:57
  228.2 0.0 copy-start
  228.2 32.4 %all-gather.6.cloned.1.call-done = bf16[256,3696]{1,0:T(8,128)(2,1)} async-done(((bf16[16,3696]{1,0:T(8,128)(2,1)}), bf16[256,3696]{1,0:T(8,128)(2,1)}) %all-gather.6.cloned.1.call-update) | async-done | bytes 1892368 | tf_op jit(solution)/shard_map/all_gather | solution.py:49
  260.6 4.6 %convolution_add_fusion = f32[256,512]{1,0:T(8,128)} fusion(f32[256,512]{1,0:T(8,128)S(1)} %fusion.6, bf16[256,3696]{1,0:T(8,128)(2,1)} %all-gather.6.cloned.1.call-done, bf16[512,3696]{0,1:T(8,128)(2,1)} %param.10), kind=kOutput, calls=%fused_computation.6 | convolution fusion | flops 969015296 | bytes 6725632 | tf_op jit(solution)/shard_map/dot_general | solution.py:60
  265.2 0.0 reduce-scatter.5.cloned.1.call-update
  265.2 0.0 copy-done
  265.2 0.0 copy-start.1
  265.2 3.1 fusion
  268.3 0.0 copy-done.1
  268.3 3.1 fusion.1
  271.4 25.2 %all-gather.8.cloned.1.call-done = bf16[256,3696]{1,0:T(8,128)(2,1)} async-done(((bf16[16,3696]{1,0:T(8,128)(2,1)}), bf16[256,3696]{1,0:T(8,128)(2,1)}) %all-gather.8.cloned.1.call-update) | async-done | bytes 1892368 | tf_op jit(solution)/shard_map/all_gather | solution.py:47
  296.6 4.6 %convolution_convert_fusion = bf16[3696,512]{1,0:T(8,128)(2,1)} fusion(bf16[256,3696]{1,0:T(8,128)(2,1)} %all-gather.8.cloned.1.call-done, bf16[256,512]{1,0:T(8,128)(2,1)S(1)} %all_gather.16), kind=kOutput, calls=%fused_computation.1 | convolution fusion | flops 970776576 | bytes 5939200 | tf_op jit(solution)/shard_map/dot_general | solution.py:54
  301.2 67.8 %reduce-scatter.5.cloned.1.call-done = f32[32,512]{1,0:T(8,128)} async-done(((f32[256,512]{1,0:T(8,128)}), f32[32,512]{1,0:T(8,128)}) %reduce-scatter.5.cloned.1.call-update) | async-done | bytes 65552 | tf_op jit(solution)/shard_map/reduce_scatter | solution.py:63
Async XLA Ops:
  7.2 178.8 %reduce-scatter.7.cloned.1.call-start = ((), (), s32[]{:S(2)}) async-start(), calls=%async_computation.6 | async-start | bytes 12115968 | tf_op jit(solution)/shard_map/reduce_scatter | solution.py:38
  37.8 3.4 copy-start.3
  41.2 1.2 copy-start.4
  41.2 29.9 %copy-start.2 = (bf16[3696,512]{1,0:T(8,128)(2,1)S(1)}, bf16[3696,512]{1,0:T(8,128)(2,1)}, u32[]{:S(2)}) copy-start(bf16[3696,512]{1,0:T(8,128)(2,1)} %param.11) | copy-start | bytes 11354116
  95.0 0.7 copy-start.5
  95.1 129.3 %all-gather.4.cloned.1.call-start = ((), (), s32[]{:S(2)}) async-start(), calls=%async_computation.2 | async-start | bytes 2019328 | tf_op jit(solution)/shard_map/all_gather | solution.py:48
  188.0 72.5 %all-gather.6.cloned.1.call-start = ((), (), s32[]{:S(2)}) async-start(), calls=%async_computation.3 | async-start | bytes 2019328 | tf_op jit(solution)/shard_map/all_gather | solution.py:49
  188.8 107.8 %all-gather.8.cloned.1.call-start = ((), (), s32[]{:S(2)}) async-start(), calls=%async_computation.5 | async-start | bytes 2019328 | tf_op jit(solution)/shard_map/all_gather | solution.py:47
  189.4 179.6 %reduce-scatter.5.cloned.1.call-start = ((), (), s32[]{:S(2)}) async-start(), calls=%async_computation.4 | async-start | bytes 589824 | tf_op jit(solution)/shard_map/reduce_scatter | solution.py:63
  228.2 37.0 %copy-start = (bf16[256,3696]{1,0:T(8,128)(2,1)S(1)}, bf16[256,3696]{1,0:T(8,128)(2,1)}, u32[]{:S(2)}) copy-start(bf16[256,3696]{1,0:T(8,128)(2,1)} %all-gather.4.cloned.1.call-done) | copy-start | bytes 5677060
  265.2 3.1 copy-start.1
Sparse Core Ops, SparseCore 0:
  95.2 90.7 reduce-scatter.6
  188.3 36.0 all-gather.3
  226.8 33.7 all-gather.5
  262.8 33.7 all-gather.7
  301.0 67.9 reduce-scatter.4
where the time goes:
time: 377 us; the launch traced here: 375 us
  waiting for transfers between devices  252 us (67%)
  blocking collectives  59.3 us (16%)
  matrix products  24.9 us (7%)
  between operations  13.9 us (4%)
  other arithmetic  12.9 us (3%)
  local copies, waits for them, and re-layouts  12.6 us (3%)
    reduce_scatter x1, waiting for transfers between devices, body(): lax.psum_scatter(jnp.concatenate([gate_part, up_part, back_part], axis=1)...  90.1 us
    reduce_scatter x1, waiting for transfers between devices, body(): lax.psum_scatter(rows_in, 'col', scatter_dimension=0, tiled=True)  67.8 us
    all_gather x1, waiting for transfers between devices, body(): gate_piece = lax.all_gather(gate_back, 'row', axis=0, tiled=True)  34.8 us
    all_gather x1, waiting for transfers between devices, body(): up_piece = lax.all_gather(up_back, 'row', axis=0, tiled=True)  32.4 us
    all_gather x1, blocking collectives, body(): lax.all_gather(tokens, 'col', axis=0, tiled=True)  30.5 us
    all_gather x1, blocking collectives, body(): lax.all_gather(out_grad, 'col', axis=0, tiled=True)  28.7 us
    all_gather x1, waiting for transfers between devices, body(): hidden_piece = lax.all_gather(weighted_hidden, 'row', axis=0, tiled=True)  25.2 us
    unnamed x13, local copies, waits for them, and re-layouts  12.5 us
  transfers between devices with their start and end apart: 5, of which 5 were waited for; matrix products, arithmetic and copies ran while one was open for 5% of the time, Pallas kernels for 0%

commit v1 on v0

v1 whole, which is shorter than its diff:
```python
import functools

import jax
import jax.numpy as jnp
from jax import lax
from jax.experimental import pallas as pl
from jax.experimental.pallas import tpu as pltpu
from jax.sharding import PartitionSpec as P

BF16, F32 = jnp.bfloat16, jnp.float32
MESH = pl.DeviceIdType.MESH
LANE = 128
TILES = (2, 4, 4, 4, 4, 4, 4, 3)
GATHER = ("zx",) * len(TILES)
LAST = 8
ORDER = sorted(
    ((s, j) for j in range(len(TILES)) for s in range(LAST + 1)),
    key=lambda e: (e[1] * 4.4 + e[0] * 2.0, -e[0]),
)
NT = (((1,), (1,)), ((), ()))


def chunks_of(width):
    assert sum(TILES) == pl.cdiv(width, LANE)
    out, at = [], 0
    for t in TILES:
        out.append((at * LANE, t * LANE, min(t * LANE, width - at * LANE)))
        at += t
    return out


(PAIR, ZA, ZB, ZUP, ZDOWN, X1, GUP, GDOWN, FUP, FDOWN, XA, XB, XC, XD, CA, CB) = range(16)
PER_CHUNK = 16
COLS = 9 + 8


def exchange_kernel(
    width,
    tok, og, tw, wg_h, wu_h, wd_h,
    r_out, ab_out, ig_out,
    wg, wu, wd, ab, pf, pr, zs1, zr1, zs2, zr2, own, xs, xr, res, rt, ig, igs, igr,
    ssem, rsem, lsem, osem,
):
    chunks = chunks_of(width)
    n = len(chunks)
    row, k = lax.axis_index("row"), lax.axis_index("col")
    x, z, c = row // 8, (row // 2) % 4, row % 2
    y, h = k // 2, k % 2
    zp, zm, zo = (z + 1) % 4, (z + 3) % 4, (z + 2) % 4
    yp, ym, yo = (y + 1) % 4, (y + 3) % 4, (y + 2) % 4

    def rdev(xx, zz, cc):
        return (xx * 8 + zz * 2 + cc, k)

    def cdev(yy, hh):
        return (row, yy * 2 + hh)

    sib, xn = rdev(x, z, 1 - c), rdev(1 - x, z, c)
    up, down = rdev(x, zp, c), rdev(x, zm, c)

    sent = []

    def send(src, dst, idx, dev):
        copy = pltpu.make_async_remote_copy(
            src_ref=src, dst_ref=dst, send_sem=ssem.at[idx], recv_sem=rsem.at[idx],
            device_id=dev, device_id_type=MESH,
        )
        copy.start()
        sent.append(copy)

    def landed(ref, idx):
        pltpu.make_async_remote_copy(
            src_ref=ref, dst_ref=ref, send_sem=ssem.at[idx], recv_sem=rsem.at[idx],
            device_id=sib, device_id_type=MESH,
        ).wait_recv()

    mine = pl.ds(pl.multiple_of(k * 32, 32), 32)
    first = [
        pltpu.make_async_copy(tok, ab.at[0, mine], lsem.at[0]),
        pltpu.make_async_copy(og, ab.at[1, mine], lsem.at[1]),
    ]
    weights = [
        pltpu.make_async_copy(wg_h, wg, lsem.at[2]),
        pltpu.make_async_copy(wu_h, wu, lsem.at[3]),
        pltpu.make_async_copy(wd_h, wd, lsem.at[4]),
    ]
    for copy in first + weights:
        copy.start()

    barrier = pltpu.get_barrier_semaphore()
    greeted = [sib, xn, up, down]
    for step in range(1, 8):
        greeted.append((row, (k + step) % 8))
    for dev in greeted:
        pl.semaphore_signal(barrier, inc=1, device_id=dev, device_id_type=MESH)
    for copy in first:
        copy.wait()
    pl.semaphore_wait(barrier, len(greeted))

    base = n * PER_CHUNK

    def block(yy, hh):
        return pl.ds(pl.multiple_of((yy * 2 + hh) * 32, 32), 32)

    def both(yy, hh):
        return ab.at[:, block(yy, hh)]

    def one(part, yy, hh):
        return ab.at[part, block(yy, hh)]

    me = both(y, h)
    send(me, me, base + 2, cdev(y, 1 - h))
    send(me, me, base + 0, cdev(yp, h))
    send(me, me, base + 1, cdev(ym, h))
    landed(both(ym, h), base + 0)
    send(one(0, ym, h), one(0, ym, h), base + 5, cdev(yp, h))
    landed(both(yp, h), base + 1)
    send(one(1, yp, h), one(1, yp, h), base + 6, cdev(ym, h))
    landed(both(y, 1 - h), base + 2)
    send(both(y, 1 - h), both(y, 1 - h), base + 3, cdev(yp, h))
    send(both(y, 1 - h), both(y, 1 - h), base + 4, cdev(ym, h))
    landed(both(ym, 1 - h), base + 3)
    send(one(0, ym, 1 - h), one(0, ym, 1 - h), base + 7, cdev(yp, h))
    landed(both(yp, 1 - h), base + 4)
    send(one(1, yp, 1 - h), one(1, yp, 1 - h), base + 8, cdev(ym, h))
    landed(one(0, yo, h), base + 5)
    landed(one(1, yo, h), base + 6)
    landed(one(0, yo, 1 - h), base + 7)
    landed(one(1, yo, 1 - h), base + 8)
    outs = [pltpu.make_async_copy(ab, ab_out, osem.at[0])]
    outs[0].start()
    for copy in weights:
        copy.wait()

    first_token = c * 128 + x * 64 + z * 16
    lanes = lax.broadcasted_iota(jnp.int32, (16, 256), 1)
    rows = lax.broadcasted_iota(jnp.int32, (16, 256), 0)
    column = jnp.sum(
        jnp.where(lanes == rows + first_token, jnp.broadcast_to(tw[...], (16, 256)), 0.0),
        axis=1, keepdims=True,
    )

    def span(j):
        o, w, _ = chunks[j]
        return slice(3 * o, 3 * o + 3 * w)

    def halves(j):
        o, w, _ = chunks[j]
        cut = 3 * o + (3 * w // LANE // 2) * LANE
        return slice(3 * o, cut), slice(cut, 3 * o + 3 * w)

    def products(j):
        o, w, valid = chunks[j]
        for part in range(3):
            for at in range(0, valid, 256):
                size = min(256, valid - at)
                lo = o + at
                value = lax.dot_general(
                    ab[part // 2], (wg, wu, wd)[part][lo : lo + size, :], NT,
                    preferred_element_type=F32,
                )
                to = 3 * o + part * w + at
                pf[:, :, :, :, to : to + size] = value.reshape(2, 2, 4, 16, size)
            if valid < w:
                pad = slice(3 * o + part * w + valid, 3 * o + part * w + w)
                pf[:, :, :, :, pad] = jnp.zeros((2, 2, 4, 16, w - valid), F32)
        cols = span(j)
        send(
            pf.at[1 - c, :, :, :, cols], pr.at[:, :, :, cols], j * PER_CHUNK + PAIR, sib
        )

    def chip(xx, zz, cols):
        return pf[c, xx, zz, :, cols] + pr[xx, zz, :, cols]

    def reduce_far(j):
        m, cols = j * PER_CHUNK, span(j)
        landed(pr.at[:, :, :, cols], m + PAIR)
        zs1[0, :, cols] = chip(0, zo, cols).astype(BF16)
        send(zs1.at[0, :, cols], zr1.at[0, :, cols], m + ZA, up)
        zs1[1, :, cols] = chip(1, zo, cols).astype(BF16)
        send(zs1.at[1, :, cols], zr1.at[1, :, cols], m + ZB, down)

    def reduce_near(j):
        m, cols = j * PER_CHUNK, span(j)
        landed(zr1.at[0, :, cols], m + ZA)
        zs2[0, 0, :, cols] = (chip(0, zp, cols) + zr1[0, :, cols].astype(F32)).astype(BF16)
        zs2[0, 1, :, cols] = chip(1, zp, cols).astype(BF16)
        send(zs2.at[0, :, :, cols], zr2.at[0, :, :, cols], m + ZUP, up)
        landed(zr1.at[1, :, cols], m + ZB)
        zs2[1, 0, :, cols] = chip(0, zm, cols).astype(BF16)
        zs2[1, 1, :, cols] = (chip(1, zm, cols) + zr1[1, :, cols].astype(F32)).astype(BF16)
        send(zs2.at[1, :, :, cols], zr2.at[1, :, :, cols], m + ZDOWN, down)

    def reduce_x(j):
        m, cols = j * PER_CHUNK, span(j)
        landed(zr2.at[0, :, :, cols], m + ZUP)
        landed(zr2.at[1, :, :, cols], m + ZDOWN)

        def ring(xx):
            return chip(xx, z, cols) + zr2[0, xx, :, cols].astype(F32) + zr2[1, xx, :, cols].astype(F32)

        xs[:, cols] = ring(1 - x).astype(BF16)
        send(xs.at[:, cols], xr.at[:, cols], m + X1, xn)
        own[:, cols] = ring(x)

    def here(xx, zz, cols):
        return res.at[c, xx, zz, :, cols]

    def push(xx, zz, cols, idx, dev):
        send(here(xx, zz, cols), here(xx, zz, cols), idx, dev)

    def activate(j):
        o, w, _ = chunks[j]
        m, cols = j * PER_CHUNK, span(j)
        landed(xr.at[:, cols], m + X1)

        def total(part):
            at = slice(3 * o + part * w, 3 * o + part * w + w)
            return own[:, at] + xr[:, at].astype(F32)

        gate, linear, back = total(0), total(1), total(2)
        sig = jax.nn.sigmoid(gate)
        silu = gate * sig
        scaled = column * back
        for part, value in enumerate((
            column * (silu * linear),
            scaled * linear * sig * (1.0 + gate * (1.0 - sig)),
            scaled * silu,
        )):
            at = slice(3 * o + part * w, 3 * o + part * w + w)
            res[c, x, z, :, at] = value.astype(BF16)
        push(x, z, cols, m + GUP, up)
        push(x, z, cols, m + GDOWN, down)
        push(x, z, cols, m + XA, xn)

    def gather_near(j):
        m, cols = j * PER_CHUNK, span(j)
        lo, hi = halves(j)
        landed(here(x, zm, cols), m + GUP)
        push(x, zm, lo, m + FUP, up)
        push(x, zm, cols, m + XB, xn)
        landed(here(x, zp, cols), m + GDOWN)
        push(x, zp, hi, m + FDOWN, down)
        push(x, zp, cols, m + XC, xn)

    def gather_far(j):
        m, cols = j * PER_CHUNK, span(j)
        lo, hi = halves(j)
        landed(here(x, zo, lo), m + FUP)
        landed(here(x, zo, hi), m + FDOWN)
        push(x, zo, cols, m + XD, xn)
        part = res.at[c, x, :, :, cols]
        send(part, part, m + CA, sib)

    def gather_x(j):
        m, cols = j * PER_CHUNK, span(j)
        landed(here(1 - x, z, cols), m + XA)
        landed(here(1 - x, zm, cols), m + XB)
        landed(here(1 - x, zp, cols), m + XC)
        landed(here(1 - x, zo, cols), m + XD)
        part = res.at[c, 1 - x, :, :, cols]
        send(part, part, m + CB, sib)

    def finish(j):
        o, w, valid = chunks[j]
        m, cols = j * PER_CHUNK, span(j)
        landed(res.at[1 - c, x, :, :, cols], m + CA)
        landed(res.at[1 - c, 1 - x, :, :, cols], m + CB)
        for part, wide in ((1, wg), (2, wu)):
            at = 3 * o + part * w
            piece = res[:, :, :, :, at : at + valid].reshape(256, valid)
            value = jnp.dot(piece, wide[o : o + valid, :], preferred_element_type=F32)
            if j == 0 and part == 1:
                ig[...] = value
            else:
                ig[...] += value
        for part in range(3):
            at = 3 * o + part * w
            rt[part, o : o + w, :] = res[:, :, :, :, at : at + w].reshape(256, w).T
        copy = pltpu.make_async_copy(
            rt.at[:, o : o + w], r_out.at[:, o : o + w], osem.at[1 + j]
        )
        copy.start()
        outs.append(copy)

    stages = (
        products, reduce_far, reduce_near, reduce_x, activate,
        gather_near, gather_far, gather_x, finish,
    )
    for stage, j in ORDER:
        stages[stage](j)

    igs[...] = ig[...].astype(BF16)
    for step in range(1, 8):
        other = (k + step) % 8
        send(
            igs.at[pl.ds(pl.multiple_of(other * 32, 32), 32)], igr.at[step], base + 9 + step,
            (row, other),
        )
    total = ig[mine, :]
    for step in range(1, 8):
        landed(igr.at[step], base + 9 + step)
        total = total + igr[step].astype(F32)
    ig_out[...] = total

    for copy in sent:
        copy.wait_send()
    for copy in outs:
        copy.wait()


def exchange(tokens, out_grad, token_weight, gate_weight, up_weight, down_weight):
    width, depth = gate_weight.shape
    wide = pl.cdiv(width, LANE) * LANE
    cols = 3 * wide
    n = len(TILES)
    messages = n * PER_CHUNK + COLS
    hbm = pl.BlockSpec(memory_space=pl.ANY)
    vmem = pl.BlockSpec(memory_space=pltpu.VMEM)
    return pl.pallas_call(
        functools.partial(exchange_kernel, width),
        out_shape=(
            jax.ShapeDtypeStruct((3, wide, 256), BF16),
            jax.ShapeDtypeStruct((2, 256, depth), BF16),
            jax.ShapeDtypeStruct((32, depth), F32),
        ),
        in_specs=[hbm, hbm, vmem, hbm, hbm, hbm],
        out_specs=(hbm, hbm, vmem),
        scratch_shapes=[
            pltpu.VMEM((width, depth), BF16),
            pltpu.VMEM((width, depth), BF16),
            pltpu.VMEM((width, depth), BF16),
            pltpu.VMEM((2, 256, depth), BF16),
            pltpu.VMEM((2, 2, 4, 16, cols), F32),
            pltpu.VMEM((2, 4, 16, cols), F32),
            pltpu.VMEM((2, 16, cols), BF16),
            pltpu.VMEM((2, 16, cols), BF16),
            pltpu.VMEM((2, 2, 16, cols), BF16),
            pltpu.VMEM((2, 2, 16, cols), BF16),
            pltpu.VMEM((16, cols), F32),
            pltpu.VMEM((16, cols), BF16),
            pltpu.VMEM((16, cols), BF16),
            pltpu.VMEM((2, 2, 4, 16, cols), BF16),
            pltpu.VMEM((3, wide, 256), BF16),
            pltpu.VMEM((256, depth), F32),
            pltpu.VMEM((256, depth), BF16),
            pltpu.VMEM((8, 32, depth), BF16),
            pltpu.SemaphoreType.DMA((messages,)),
            pltpu.SemaphoreType.DMA((messages,)),
            pltpu.SemaphoreType.DMA((5,)),
            pltpu.SemaphoreType.DMA((1 + n,)),
        ],
        compiler_params=pltpu.CompilerParams(
            collective_id=0, has_side_effects=True, vmem_limit_bytes=56 * 1024 * 1024
        ),
        cost_estimate=pl.CostEstimate(
            flops=10 * 256 * depth * width, bytes_accessed=6 * depth * width + 6 * 256 * width,
            transcendentals=0,
        ),
        name="exchange",
    )(tokens, out_grad, token_weight.reshape(1, 256), gate_weight, up_weight, down_weight)


def grads_kernel(r, ab, gate_grad, up_grad, down_grad):
    for part, out in ((1, gate_grad), (2, up_grad), (0, down_grad)):
        out[...] = jnp.dot(
            r[part], ab[0 if part else 1], preferred_element_type=F32
        ).astype(BF16)


def grads(r, ab, width):
    depth = ab.shape[2]
    step = 512
    out = pl.BlockSpec((step, depth), lambda i: (i, 0))
    return pl.pallas_call(
        grads_kernel,
        grid=(pl.cdiv(width, step),),
        in_specs=[
            pl.BlockSpec((3, step, 256), lambda i: (0, i, 0)),
            pl.BlockSpec((2, 256, depth), lambda i: (0, 0, 0)),
        ],
        out_specs=(out, out, out),
        out_shape=(jax.ShapeDtypeStruct((width, depth), BF16),) * 3,
        compiler_params=pltpu.CompilerParams(vmem_limit_bytes=56 * 1024 * 1024),
        name="grads",
    )(r, ab)


def body(tokens, out_grad, token_weight, gate_weight, up_weight, down_weight):
    width = gate_weight.shape[1]
    r, ab, input_grad = exchange(
        tokens, out_grad, token_weight, gate_weight.T, up_weight.T, down_weight
    )
    gate_grad, up_grad, down_grad = grads(r, ab, width)
    return input_grad, gate_grad.T, up_grad.T, down_grad


def solution(mesh):
    return jax.shard_map(
        body,
        mesh=mesh,
        in_specs=(
            P("col", "row"),
            P("col", "row"),
            P(),
            P("row", "col"),
            P("row", "col"),
            P("col", "row"),
        ),
        out_specs=(P("col", "row"), P("row", "col"), P("row", "col"), P("col", "row")),
        check_vma=False,
    )
```

time: 377 us -> 123 us (0.33)
  waiting for transfers between devices: 252 us -> 0 us
  Pallas kernels: 0 us -> 121 us
  blocking collectives: 59.3 us -> 0 us
  matrix products: 24.9 us -> 0 us
  between operations: 13.9 us -> 0.65 us
  other arithmetic: 12.9 us -> 0 us
  local copies, waits for them, and re-layouts: 12.6 us -> 0.63 us
    reduce_scatter x2 -> x0, waiting for transfers between devices: 158 us -> none  [the longest x1 90.1 us: body(): lax.psum_scatter(jnp.concatenate([gate_part, up_part, back_part], axis=1)...]
    pallas_call x0 -> x2, Pallas kernels: none -> 121 us  [the longest x1 111 us: exchange(): pl.pallas_call(functools.partial(exchange_kernel, width), out_shape=(jax....]
    all_gather x3 -> x0, waiting for transfers between devices: 92.4 us -> none  [the longest x1 34.8 us: body(): gate_piece = lax.all_gather(gate_back, 'row', axis=0, tiled=True)]
    all_gather x2 -> x0, blocking collectives: 59.3 us -> none  [the longest x1 30.5 us: body(): lax.all_gather(tokens, 'col', axis=0, tiled=True)]
    dot_general x8 -> x0, matrix products: 24.9 us -> none  [the longest x1 4.62 us: body(): lax.dot_general(up_piece, up_weight, over_hidden, preferred_element_type=...]
    unnamed x13 -> x3, local copies, waits for them, and re-layouts: 12.5 us -> 0.63 us
    concatenate x1 -> x0, other arithmetic: 10.8 us -> none  [body(): jnp.concatenate([gate_part, up_part, back_part], axis=1)]
  transfers between devices with their start and end apart: 5 -> 0, of which waited for: 5 -> 0; matrix products, arithmetic and copies ran while one was open for 5% -> 0% of each run, Pallas kernels for 0% -> 0%
where the time goes in v1:
time: 123 us; the launch traced here: 122 us
  Pallas kernels  121 us (98%)
    pallas_call x1, Pallas kernels, exchange(): pl.pallas_call(functools.partial(exchange_kernel, width), out_shape=(jax....  111 us
    pallas_call x1, Pallas kernels, grads(): pl.pallas_call(grads_kernel, grid=(pl.cdiv(width, step),), in_specs=[pl.B...  10.3 us

profile of v1, /device:TPU:1, one launch (start us, length us, event | category | flops | bytes accessed | tf_op | source)
XLA Modules:
  0.0 122.4 jit_solution(16046881225763306147)
XLA Ops:
  0.6 110.8 %exchange.1 = (bf16[3,3712,256]{2,1,0:T(8,128)(2,1)}, bf16[2,256,512]{2,1,0:T(8,128)(2,1)}, f32[32,512]{1,0:T(8,128)}) custom-call(bf16[32,512]{1,0:T(8,128)(2,1)} %tok.1, bf16[32,512]{1,0:T(8,128)(2,1)} %og.1, f32[1,256]{1,0:T(1,128)} %bitcast.9, bf16[3696,512]{1,0:T(8,128)(2,1)} %bitcast.5, bf16[3696,512]{1,0:T(8,128)(2,1)} %bitcast.6, bf16[3696,512]{1,0:T(8,128)(2,1)} %wd_h.1), custom_call_target="tpu_custom_call" | custom-call | flops 4844421120 | bytes 17031168 | tf_op jit(solution)/shard_map/exchange/pallas_call | solution.py:320
  111.5 0.0 copy-start
  111.5 10.3 %grads.1 = (bf16[3696,512]{1,0:T(8,128)(2,1)}, bf16[3696,512]{1,0:T(8,128)(2,1)}, bf16[3696,512]{1,0:T(8,128)(2,1)}) custom-call(bf16[3,3712,256]{2,1,0:T(8,128)(2,1)} %get-tuple-element.11.r, bf16[2,256,512]{2,1,0:T(8,128)(2,1)} %get-tuple-element.12.ab), custom_call_target="tpu_custom_call" | custom-call | tf_op jit(solution)/shard_map/grads/pallas_call | solution.py:375
  121.7 0.0 copy-done
  121.7 0.6 copy.11
Async XLA Ops:
  111.5 10.3 %copy-start = (f32[32,512]{1,0:T(8,128)S(1)}, f32[32,512]{1,0:T(8,128)}, u32[]{:S(2)}) copy-start(f32[32,512]{1,0:T(8,128)} %get-tuple-element.20) | copy-start | bytes 196612

commit v2 on v1

--- a/solution.py
+++ b/solution.py
@@ -10,12 +10,16 @@
 BF16, F32 = jnp.bfloat16, jnp.float32
 MESH = pl.DeviceIdType.MESH
 LANE = 128
-TILES = (2, 4, 4, 4, 4, 4, 4, 3)
-GATHER = ("zx",) * len(TILES)
-LAST = 8
-ORDER = sorted(
-    ((s, j) for j in range(len(TILES)) for s in range(LAST + 1)),
-    key=lambda e: (e[1] * 4.4 + e[0] * 2.0, -e[0]),
+TILES = (3, 3, 4, 4, 2, 5, 4, 4)
+REDUCE = ["zx", "zx", "xz", "zx", "xz", "zx", "zx", "xz"]
+GATHER = ["xz", "xz", "zx", "zx", "xz", "xz", "zx", "xz"]
+ORDER = (
+    (0, 0), (0, 1), (0, 2), (0, 3), (0, 4), (1, 0), (0, 5), (1, 1), (0, 6), (2, 0), (1, 2), (2, 1),
+    (1, 3), (1, 4), (0, 7), (3, 0), (1, 5), (3, 1), (1, 6), (2, 3), (2, 2), (1, 7), (2, 5), (4, 0),
+    (2, 4), (4, 1), (3, 3), (3, 2), (2, 6), (3, 5), (3, 4), (2, 7), (5, 0), (4, 2), (5, 1), (4, 3),
+    (3, 6), (4, 4), (4, 5), (3, 7), (6, 0), (5, 2), (4, 6), (5, 4), (6, 1), (5, 5), (5, 3), (4, 7),
+    (7, 0), (6, 2), (5, 6), (8, 0), (6, 4), (7, 1), (5, 7), (7, 2), (8, 1), (6, 5), (6, 3), (6, 6),
+    (7, 4), (8, 2), (7, 3), (6, 7), (8, 4), (7, 6), (7, 5), (8, 3), (7, 7), (8, 6), (8, 5), (8, 7),
 )
 NT = (((1,), (1,)), ((), ()))
 
@@ -29,8 +33,10 @@
     return out
 
 
-(PAIR, ZA, ZB, ZUP, ZDOWN, X1, GUP, GDOWN, FUP, FDOWN, XA, XB, XC, XD, CA, CB) = range(16)
-PER_CHUNK = 16
+(
+    PAIR, ZA, ZB, ZUP, ZDOWN, X1, GUP, GDOWN, FUP, FDOWN, XA, XB, XC, XD, CA, CB, CC, CD,
+) = range(18)
+PER_CHUNK = 18
 COLS = 9 + 8
 
 
@@ -172,7 +178,10 @@
     def chip(xx, zz, cols):
         return pf[c, xx, zz, :, cols] + pr[xx, zz, :, cols]
 
-    def reduce_far(j):
+    def chip_sum(xx, zz, cols):
+        return chip(xx, zz, cols) + xr[zz, :, cols].astype(F32)
+
+    def zx_far(j):
         m, cols = j * PER_CHUNK, span(j)
         landed(pr.at[:, :, :, cols], m + PAIR)
         zs1[0, :, cols] = chip(0, zo, cols).astype(BF16)
@@ -180,7 +189,7 @@
         zs1[1, :, cols] = chip(1, zo, cols).astype(BF16)
         send(zs1.at[1, :, cols], zr1.at[1, :, cols], m + ZB, down)
 
-    def reduce_near(j):
+    def zx_near(j):
         m, cols = j * PER_CHUNK, span(j)
         landed(zr1.at[0, :, cols], m + ZA)
         zs2[0, 0, :, cols] = (chip(0, zp, cols) + zr1[0, :, cols].astype(F32)).astype(BF16)
@@ -191,7 +200,7 @@
         zs2[1, 1, :, cols] = (chip(1, zm, cols) + zr1[1, :, cols].astype(F32)).astype(BF16)
         send(zs2.at[1, :, :, cols], zr2.at[1, :, :, cols], m + ZDOWN, down)
 
-    def reduce_x(j):
+    def zx_cross(j):
         m, cols = j * PER_CHUNK, span(j)
         landed(zr2.at[0, :, :, cols], m + ZUP)
         landed(zr2.at[1, :, :, cols], m + ZDOWN)
@@ -199,9 +208,49 @@
         def ring(xx):
             return chip(xx, z, cols) + zr2[0, xx, :, cols].astype(F32) + zr2[1, xx, :, cols].astype(F32)
 
-        xs[:, cols] = ring(1 - x).astype(BF16)
-        send(xs.at[:, cols], xr.at[:, cols], m + X1, xn)
+        xs[0, :, cols] = ring(1 - x).astype(BF16)
+        send(xs.at[0, :, cols], xr.at[0, :, cols], m + X1, xn)
         own[:, cols] = ring(x)
+
+    def zx_total(j):
+        m, cols = j * PER_CHUNK, span(j)
+        landed(xr.at[0, :, cols], m + X1)
+        return lambda at: own[:, at] + xr[0, :, at].astype(F32)
+
+    def xz_cross(j):
+        m, cols = j * PER_CHUNK, span(j)
+        landed(pr.at[:, :, :, cols], m + PAIR)
+        xs[:, :, cols] = (pf[c, 1 - x, :, :, cols] + pr[1 - x, :, :, cols]).astype(BF16)
+        send(xs.at[:, :, cols], xr.at[:, :, cols], m + X1, xn)
+
+    def xz_far(j):
+        m, cols = j * PER_CHUNK, span(j)
+        lo, hi = halves(j)
+        landed(xr.at[:, :, cols], m + X1)
+        zs1[0, :, lo] = chip_sum(x, zo, lo).astype(BF16)
+        send(zs1.at[0, :, lo], zr1.at[0, :, lo], m + ZA, up)
+        zs1[1, :, hi] = chip_sum(x, zo, hi).astype(BF16)
+        send(zs1.at[1, :, hi], zr1.at[1, :, hi], m + ZB, down)
+
+    def xz_near(j):
+        m, cols = j * PER_CHUNK, span(j)
+        lo, hi = halves(j)
+        landed(zr1.at[0, :, lo], m + ZA)
+        zs2[0, 0, :, lo] = (chip_sum(x, zp, lo) + zr1[0, :, lo].astype(F32)).astype(BF16)
+        zs2[0, 0, :, hi] = chip_sum(x, zp, hi).astype(BF16)
+        send(zs2.at[0, 0, :, cols], zr2.at[0, 0, :, cols], m + ZUP, up)
+        landed(zr1.at[1, :, hi], m + ZB)
+        zs2[1, 0, :, lo] = chip_sum(x, zm, lo).astype(BF16)
+        zs2[1, 0, :, hi] = (chip_sum(x, zm, hi) + zr1[1, :, hi].astype(F32)).astype(BF16)
+        send(zs2.at[1, 0, :, cols], zr2.at[1, 0, :, cols], m + ZDOWN, down)
+
+    def xz_total(j):
+        m, cols = j * PER_CHUNK, span(j)
+        landed(zr2.at[0, 0, :, cols], m + ZUP)
+        landed(zr2.at[1, 0, :, cols], m + ZDOWN)
+        return lambda at: (
+            chip_sum(x, z, at) + zr2[0, 0, :, at].astype(F32) + zr2[1, 0, :, at].astype(F32)
+        )
 
     def here(xx, zz, cols):
         return res.at[c, xx, zz, :, cols]
@@ -209,16 +258,19 @@
     def push(xx, zz, cols, idx, dev):
         send(here(xx, zz, cols), here(xx, zz, cols), idx, dev)
 
+    def push_pair(zz, cols, idx, dev):
+        part = res.at[c, :, zz, :, cols]
+        send(part, part, idx, dev)
+
     def activate(j):
         o, w, _ = chunks[j]
         m, cols = j * PER_CHUNK, span(j)
-        landed(xr.at[:, cols], m + X1)
-
-        def total(part):
-            at = slice(3 * o + part * w, 3 * o + part * w + w)
-            return own[:, at] + xr[:, at].astype(F32)
-
-        gate, linear, back = total(0), total(1), total(2)
+        total = (xz_total if REDUCE[j] == "xz" else zx_total)(j)
+
+        def place(part):
+            return slice(3 * o + part * w, 3 * o + part * w + w)
+
+        gate, linear, back = total(place(0)), total(place(1)), total(place(2))
         sig = jax.nn.sigmoid(gate)
         silu = gate * sig
         scaled = column * back
@@ -227,13 +279,13 @@
             scaled * linear * sig * (1.0 + gate * (1.0 - sig)),
             scaled * silu,
         )):
-            at = slice(3 * o + part * w, 3 * o + part * w + w)
-            res[c, x, z, :, at] = value.astype(BF16)
-        push(x, z, cols, m + GUP, up)
-        push(x, z, cols, m + GDOWN, down)
+            res[c, x, z, :, place(part)] = value.astype(BF16)
         push(x, z, cols, m + XA, xn)
-
-    def gather_near(j):
+        if GATHER[j] == "zx":
+            push(x, z, cols, m + GUP, up)
+            push(x, z, cols, m + GDOWN, down)
+
+    def zx_gather_near(j):
         m, cols = j * PER_CHUNK, span(j)
         lo, hi = halves(j)
         landed(here(x, zm, cols), m + GUP)
@@ -243,7 +295,7 @@
         push(x, zp, hi, m + FDOWN, down)
         push(x, zp, cols, m + XC, xn)
 
-    def gather_far(j):
+    def zx_gather_far(j):
         m, cols = j * PER_CHUNK, span(j)
         lo, hi = halves(j)
         landed(here(x, zo, lo), m + FUP)
@@ -252,7 +304,7 @@
         part = res.at[c, x, :, :, cols]
         send(part, part, m + CA, sib)
 
-    def gather_x(j):
+    def zx_gather_cross(j):
         m, cols = j * PER_CHUNK, span(j)
         landed(here(1 - x, z, cols), m + XA)
         landed(here(1 - x, zm, cols), m + XB)
@@ -261,11 +313,42 @@
         part = res.at[c, 1 - x, :, :, cols]
         send(part, part, m + CB, sib)
 
+    def zx_all(j):
+        m, cols = j * PER_CHUNK, span(j)
+        landed(res.at[1 - c, x, :, :, cols], m + CA)
+        landed(res.at[1 - c, 1 - x, :, :, cols], m + CB)
+
+    def xz_gather_cross(j):
+        m, cols = j * PER_CHUNK, span(j)
+        landed(here(1 - x, z, cols), m + XA)
+        push_pair(z, cols, m + GUP, up)
+        push_pair(z, cols, m + GDOWN, down)
+        push_pair(z, cols, m + CA, sib)
+
+    def xz_gather_near(j):
+        m, cols = j * PER_CHUNK, span(j)
+        landed(res.at[c, :, zm, :, cols], m + GUP)
+        push(0, zm, cols, m + FUP, up)
+        landed(res.at[c, :, zp, :, cols], m + GDOWN)
+        push(1, zp, cols, m + FDOWN, down)
+        push_pair(zm, cols, m + CB, sib)
+        push_pair(zp, cols, m + CC, sib)
+
+    def xz_gather_far(j):
+        m, cols = j * PER_CHUNK, span(j)
+        landed(here(0, zo, cols), m + FUP)
+        landed(here(1, zo, cols), m + FDOWN)
+        push_pair(zo, cols, m + CD, sib)
+
+    def xz_all(j):
+        m, cols = j * PER_CHUNK, span(j)
+        for zz, idx in ((z, CA), (zm, CB), (zp, CC), (zo, CD)):
+            landed(res.at[1 - c, :, zz, :, cols], m + idx)
+
     def finish(j):
         o, w, valid = chunks[j]
         m, cols = j * PER_CHUNK, span(j)
-        landed(res.at[1 - c, x, :, :, cols], m + CA)
-        landed(res.at[1 - c, 1 - x, :, :, cols], m + CB)
+        (zx_all if GATHER[j] == "zx" else xz_all)(j)
         for part, wide in ((1, wg), (2, wu)):
             at = 3 * o + part * w
             piece = res[:, :, :, :, at : at + valid].reshape(256, valid)
@@ -283,12 +366,13 @@
         copy.start()
         outs.append(copy)
 
-    stages = (
-        products, reduce_far, reduce_near, reduce_x, activate,
-        gather_near, gather_far, gather_x, finish,
-    )
+    reduce = {"zx": (zx_far, zx_near, zx_cross), "xz": (xz_cross, xz_far, xz_near)}
+    gather = {
+        "zx": (zx_gather_near, zx_gather_far, zx_gather_cross),
+        "xz": (xz_gather_cross, xz_gather_near, xz_gather_far),
+    }
     for stage, j in ORDER:
-        stages[stage](j)
+        (products, *reduce[REDUCE[j]], activate, *gather[GATHER[j]], finish)[stage](j)
 
     igs[...] = ig[...].astype(BF16)
     for step in range(1, 8):
@@ -338,8 +422,8 @@
             pltpu.VMEM((2, 2, 16, cols), BF16),
             pltpu.VMEM((2, 2, 16, cols), BF16),
             pltpu.VMEM((16, cols), F32),
-            pltpu.VMEM((16, cols), BF16),
-            pltpu.VMEM((16, cols), BF16),
+            pltpu.VMEM((4, 16, cols), BF16),
+            pltpu.VMEM((4, 16, cols), BF16),
             pltpu.VMEM((2, 2, 4, 16, cols), BF16),
             pltpu.VMEM((3, wide, 256), BF16),
             pltpu.VMEM((256, depth), F32),

time: 123 us -> 90.4 us (0.73)
  Pallas kernels: 121 us -> 88.8 us
    pallas_call x1, Pallas kernels: 111 us -> 78.6 us  [exchange(): pl.pallas_call(functools.partial(exchange_kernel, width), out_shape=(jax....]
where the time goes in v2:
time: 90.4 us; the launch traced here: 90.1 us
  Pallas kernels  88.8 us (98%)
    pallas_call x1, Pallas kernels, exchange(): pl.pallas_call(functools.partial(exchange_kernel, width), out_shape=(jax....  78.6 us
    pallas_call x1, Pallas kernels, grads(): pl.pallas_call(grads_kernel, grid=(pl.cdiv(width, step),), in_specs=[pl.B...  10.3 us

profile of v2, /device:TPU:1, one launch (start us, length us, event | category | flops | bytes accessed | tf_op | source)
XLA Modules:
  0.0 90.1 jit_solution(18127756424019137394)
XLA Ops:
  0.6 78.6 %exchange.1 = (bf16[3,3712,256]{2,1,0:T(8,128)(2,1)}, bf16[2,256,512]{2,1,0:T(8,128)(2,1)}, f32[32,512]{1,0:T(8,128)}) custom-call(bf16[32,512]{1,0:T(8,128)(2,1)} %tok.1, bf16[32,512]{1,0:T(8,128)(2,1)} %og.1, f32[1,256]{1,0:T(1,128)} %bitcast.9, bf16[3696,512]{1,0:T(8,128)(2,1)} %bitcast.5, bf16[3696,512]{1,0:T(8,128)(2,1)} %bitcast.6, bf16[3696,512]{1,0:T(8,128)(2,1)} %wd_h.1), custom_call_target="tpu_custom_call" | custom-call | flops 4844421120 | bytes 17031168 | tf_op jit(solution)/shard_map/exchange/pallas_call | solution.py:404
  79.2 0.0 copy-start
  79.2 10.3 %grads.1 = (bf16[3696,512]{1,0:T(8,128)(2,1)}, bf16[3696,512]{1,0:T(8,128)(2,1)}, bf16[3696,512]{1,0:T(8,128)(2,1)}) custom-call(bf16[3,3712,256]{2,1,0:T(8,128)(2,1)} %get-tuple-element.11.r, bf16[2,256,512]{2,1,0:T(8,128)(2,1)} %get-tuple-element.12.ab), custom_call_target="tpu_custom_call" | custom-call | tf_op jit(solution)/shard_map/grads/pallas_call | solution.py:459
  89.5 0.0 copy-done
  89.5 0.6 copy.11
Async XLA Ops:
  79.2 10.3 %copy-start = (f32[32,512]{1,0:T(8,128)S(1)}, f32[32,512]{1,0:T(8,128)}, u32[]{:S(2)}) copy-start(f32[32,512]{1,0:T(8,128)} %get-tuple-element.20) | copy-start | bytes 196612

commit v3 on v2

--- a/solution.py
+++ b/solution.py
@@ -404,8 +404,8 @@
     return pl.pallas_call(
         functools.partial(exchange_kernel, width),
         out_shape=(
-            jax.ShapeDtypeStruct((3, wide, 256), BF16),
-            jax.ShapeDtypeStruct((2, 256, depth), BF16),
+            pltpu.VMEM((3, wide, 256), BF16),
+            pltpu.VMEM((2, 256, depth), BF16),
             jax.ShapeDtypeStruct((32, depth), F32),
         ),
         in_specs=[hbm, hbm, vmem, hbm, hbm, hbm],
@@ -435,7 +435,7 @@
             pltpu.SemaphoreType.DMA((1 + n,)),
         ],
         compiler_params=pltpu.CompilerParams(
-            collective_id=0, has_side_effects=True, vmem_limit_bytes=56 * 1024 * 1024
+            collective_id=0, has_side_effects=True, vmem_limit_bytes=50 * 1024 * 1024
         ),
         cost_estimate=pl.CostEstimate(
             flops=10 * 256 * depth * width, bytes_accessed=6 * depth * width + 6 * 256 * width,
@@ -454,7 +454,7 @@
 
 def grads(r, ab, width):
     depth = ab.shape[2]
-    step = 512
+    step = 528
     out = pl.BlockSpec((step, depth), lambda i: (i, 0))
     return pl.pallas_call(
         grads_kernel,
@@ -465,7 +465,7 @@
         ],
         out_specs=(out, out, out),
         out_shape=(jax.ShapeDtypeStruct((width, depth), BF16),) * 3,
-        compiler_params=pltpu.CompilerParams(vmem_limit_bytes=56 * 1024 * 1024),
+        compiler_params=pltpu.CompilerParams(vmem_limit_bytes=16 * 1024 * 1024),
         name="grads",
     )(r, ab)
 

time: 90.4 us -> 86.4 us (0.956)
  Pallas kernels: 88.8 us -> 84.9 us
    pallas_call x1, Pallas kernels: 10.3 us -> 6.68 us  [grads(): pl.pallas_call(grads_kernel, grid=(pl.cdiv(width, step),), in_specs=[pl.B...]
where the time goes in v3:
time: 86.4 us; the launch traced here: 86.2 us
  Pallas kernels  84.9 us (98%)
    pallas_call x1, Pallas kernels, exchange(): pl.pallas_call(functools.partial(exchange_kernel, width), out_shape=(pltp...  78.2 us
    pallas_call x1, Pallas kernels, grads(): pl.pallas_call(grads_kernel, grid=(pl.cdiv(width, step),), in_specs=[pl.B...  6.68 us

profile of v3, /device:TPU:1, one launch (start us, length us, event | category | flops | bytes accessed | tf_op | source)
XLA Modules:
  0.0 86.2 jit_solution(14095734082962739152)
XLA Ops:
  0.6 78.2 %exchange.1 = (bf16[3,3712,256]{2,1,0:T(8,128)(2,1)S(1)}, bf16[2,256,512]{2,1,0:T(8,128)(2,1)S(1)}, f32[32,512]{1,0:T(8,128)}) custom-call(bf16[32,512]{1,0:T(8,128)(2,1)} %tok.1, bf16[32,512]{1,0:T(8,128)(2,1)} %og.1, f32[1,256]{1,0:T(1,128)} %bitcast.9, bf16[3696,512]{1,0:T(8,128)(2,1)} %bitcast.5, bf16[3696,512]{1,0:T(8,128)(2,1)} %bitcast.6, ...), custom_call_target="tpu_custom_call" | custom-call | flops 4844421120 | bytes 17031168 | tf_op jit(solution)/shard_map/exchange/pallas_call | solution.py:404
  78.9 0.0 copy-start
  78.9 6.7 %grads.1 = (bf16[3696,512]{1,0:T(8,128)(2,1)}, bf16[3696,512]{1,0:T(8,128)(2,1)}, bf16[3696,512]{1,0:T(8,128)(2,1)}) custom-call(bf16[3,3712,256]{2,1,0:T(8,128)(2,1)S(1)} %get-tuple-element.11.r, bf16[2,256,512]{2,1,0:T(8,128)(2,1)S(1)} %get-tuple-element.12.ab), custom_call_target="tpu_custom_call" | custom-call | tf_op jit(solution)/shard_map/grads/pallas_call | solution.py:459
  85.6 0.0 copy-done
  85.6 0.6 copy.11
Async XLA Ops:
  78.9 6.7 %copy-start = (f32[32,512]{1,0:T(8,128)S(1)}, f32[32,512]{1,0:T(8,128)}, u32[]{:S(2)}) copy-start(f32[32,512]{1,0:T(8,128)} %get-tuple-element.20) | copy-start | bytes 196612

commit v4 on v3

--- a/solution.py
+++ b/solution.py
@@ -37,16 +37,20 @@
     PAIR, ZA, ZB, ZUP, ZDOWN, X1, GUP, GDOWN, FUP, FDOWN, XA, XB, XC, XD, CA, CB, CC, CD,
 ) = range(18)
 PER_CHUNK = 18
-COLS = 9 + 8
+STEPS = ((1, 0), (3, 0), (0, 1), (2, 0), (1, 1), (3, 1), (2, 1))
+COLS = 9
 
 
 def exchange_kernel(
     width,
     tok, og, tw, wg_h, wu_h, wd_h,
-    r_out, ab_out, ig_out,
-    wg, wu, wd, ab, pf, pr, zs1, zr1, zs2, zr2, own, xs, xr, res, rt, ig, igs, igr,
-    ssem, rsem, lsem, osem,
+    r_out, ab_out, ig_own, *rest,
 ):
+    ig_send = rest[:7]
+    (
+        wg, wu, wd, ab, pf, pr, zs1, zr1, zs2, zr2, own, xs, xr, res, rt, ig,
+        ssem, rsem, lsem, osem,
+    ) = rest[7:]
     chunks = chunks_of(width)
     n = len(chunks)
     row, k = lax.axis_index("row"), lax.axis_index("col")
@@ -94,9 +98,7 @@
         copy.start()
 
     barrier = pltpu.get_barrier_semaphore()
-    greeted = [sib, xn, up, down]
-    for step in range(1, 8):
-        greeted.append((row, (k + step) % 8))
+    greeted = [sib, xn, up, down, cdev(yp, h), cdev(ym, h), cdev(y, 1 - h)]
     for dev in greeted:
         pl.semaphore_signal(barrier, inc=1, device_id=dev, device_id_type=MESH)
     for copy in first:
@@ -374,18 +376,9 @@
     for stage, j in ORDER:
         (products, *reduce[REDUCE[j]], activate, *gather[GATHER[j]], finish)[stage](j)
 
-    igs[...] = ig[...].astype(BF16)
-    for step in range(1, 8):
-        other = (k + step) % 8
-        send(
-            igs.at[pl.ds(pl.multiple_of(other * 32, 32), 32)], igr.at[step], base + 9 + step,
-            (row, other),
-        )
-    total = ig[mine, :]
-    for step in range(1, 8):
-        landed(igr.at[step], base + 9 + step)
-        total = total + igr[step].astype(F32)
-    ig_out[...] = total
+    ig_own[...] = ig[mine, :]
+    for share, (dy, dh) in zip(ig_send, STEPS):
+        share[...] = ig[block((y + dy) % 4, (h + dh) % 2), :].astype(BF16)
 
     for copy in sent:
         copy.wait_send()
@@ -407,9 +400,10 @@
             pltpu.VMEM((3, wide, 256), BF16),
             pltpu.VMEM((2, 256, depth), BF16),
             jax.ShapeDtypeStruct((32, depth), F32),
+            *(jax.ShapeDtypeStruct((32, depth), BF16),) * 7,
         ),
         in_specs=[hbm, hbm, vmem, hbm, hbm, hbm],
-        out_specs=(hbm, hbm, vmem),
+        out_specs=(hbm, hbm) + (vmem,) * 8,
         scratch_shapes=[
             pltpu.VMEM((width, depth), BF16),
             pltpu.VMEM((width, depth), BF16),
@@ -427,8 +421,6 @@
             pltpu.VMEM((2, 2, 4, 16, cols), BF16),
             pltpu.VMEM((3, wide, 256), BF16),
             pltpu.VMEM((256, depth), F32),
-            pltpu.VMEM((256, depth), BF16),
-            pltpu.VMEM((8, 32, depth), BF16),
             pltpu.SemaphoreType.DMA((messages,)),
             pltpu.SemaphoreType.DMA((messages,)),
             pltpu.SemaphoreType.DMA((5,)),
@@ -466,16 +458,28 @@
         out_specs=(out, out, out),
         out_shape=(jax.ShapeDtypeStruct((width, depth), BF16),) * 3,
         compiler_params=pltpu.CompilerParams(vmem_limit_bytes=16 * 1024 * 1024),
+        cost_estimate=pl.CostEstimate(
+            flops=6 * 256 * depth * width, bytes_accessed=6 * depth * width, transcendentals=0
+        ),
         name="grads",
     )(r, ab)
 
 
 def body(tokens, out_grad, token_weight, gate_weight, up_weight, down_weight):
     width = gate_weight.shape[1]
-    r, ab, input_grad = exchange(
+    r, ab, input_grad, *shares = exchange(
         tokens, out_grad, token_weight, gate_weight.T, up_weight.T, down_weight
     )
+    shares = [
+        lax.ppermute(
+            share, "col",
+            [(y * 2 + h, (y + dy) % 4 * 2 + (h + dh) % 2) for y in range(4) for h in range(2)],
+        )
+        for share, (dy, dh) in zip(shares, STEPS)
+    ]
     gate_grad, up_grad, down_grad = grads(r, ab, width)
+    for share in shares:
+        input_grad = input_grad + share.astype(F32)
     return input_grad, gate_grad.T, up_grad.T, down_grad
 
 

time: 86.4 us -> 92.5 us (1.071)
  starting transfers between devices: 0 us -> 12.3 us
  Pallas kernels: 84.9 us -> 77.9 us
    ppermute x0 -> x7, starting transfers between devices: none -> 12.3 us  [body(): lax.ppermute(share, 'col', [(y * 2 + h, (y + dy) % 4 * 2 + (h + dh) % 2)...]
    pallas_call x1, Pallas kernels: 78.2 us -> 71.3 us  [exchange(): pl.pallas_call(functools.partial(exchange_kernel, width), out_shape=(pltp...]
  transfers between devices with their start and end apart: 0 -> 7, of which waited for: 0 -> 0; matrix products, arithmetic and copies ran while one was open for 0% -> 0% of each run, Pallas kernels for 0% -> 7%
where the time goes in v4:
time: 92.5 us; the launch traced here: 91.6 us
  Pallas kernels  77.9 us (84%)
  starting transfers between devices  12.3 us (13%)
    pallas_call x1, Pallas kernels, exchange(): pl.pallas_call(functools.partial(exchange_kernel, width), out_shape=(pltp...  71.3 us
    ppermute x7, starting transfers between devices, body(): lax.ppermute(share, 'col', [(y * 2 + h, (y + dy) % 4 * 2 + (h + dh) % 2)...  12.3 us
    pallas_call x1, Pallas kernels, grads(): pl.pallas_call(grads_kernel, grid=(pl.cdiv(width, step),), in_specs=[pl.B...  6.65 us
  transfers between devices with their start and end apart: 7, of which 0 were waited for; matrix products, arithmetic and copies ran while one was open for 0% of the time, Pallas kernels for 7%

profile of v4, /device:TPU:1, one launch (start us, length us, event | category | flops | bytes accessed | tf_op | source)
XLA Modules:
  0.0 91.6 jit_solution(11506378985589474667)
XLA Ops:
  0.6 71.3 %exchange.1 = (bf16[3,3712,256]{2,1,0:T(8,128)(2,1)S(1)}, bf16[2,256,512]{2,1,0:T(8,128)(2,1)S(1)}, f32[32,512]{1,0:T(8,128)}, bf16[32,512]{1,0:T(8,128)(2,1)}, ...) custom-call(bf16[32,512]{1,0:T(8,128)(2,1)} %tok.1, ...), custom_call_target="tpu_custom_call" | custom-call | flops 4844421120 | bytes 17031168 | tf_op jit(solution)/shard_map/exchange/pallas_call | solution.py:397
  71.9 1.0 %collective-permute-start = (bf16[32,512]{1,0:T(8,128)(2,1)}, bf16[32,512]{1,0:T(8,128)(2,1)S(1)}, u32[]{:S(2)}, u32[]{:S(2)}) collective-permute-start(bf16[32,512]{1,0:T(8,128)(2,1)} %get-tuple-element.18), channel_id=1, source_target_pairs={{0,2},{1,3},{2,4},{3,5},{4,6},{5,7},{6,0},{7,1},{8,10},{9,11},{10,... | collective-permute-start | bytes 98312 | tf_op jit(solution)/shard_map/ppermute | solution.py:474
  72.9 1.8 %collective-permute-start.1 = (bf16[32,512]{1,0:T(8,128)(2,1)}, bf16[32,512]{1,0:T(8,128)(2,1)S(1)}, u32[]{:S(2)}, u32[]{:S(2)}) collective-permute-start(bf16[32,512]{1,0:T(8,128)(2,1)} %get-tuple-element.19), channel_id=1, source_target_pairs={{0,6},{1,7},{2,0},{3,1},{4,2},{5,3},{6,4},{7,5},{8,14},{9,15},{10,... | collective-permute-start | bytes 98312 | tf_op jit(solution)/shard_map/ppermute | solution.py:474
  74.7 2.3 %collective-permute-start.2 = (bf16[32,512]{1,0:T(8,128)(2,1)}, bf16[32,512]{1,0:T(8,128)(2,1)S(1)}, u32[]{:S(2)}, u32[]{:S(2)}) collective-permute-start(bf16[32,512]{1,0:T(8,128)(2,1)} %get-tuple-element.20), channel_id=1, source_target_pairs={{0,1},{1,0},{2,3},{3,2},{4,5},{5,4},{6,7},{7,6},{8,9},{9,8},{10,11... | collective-permute-start | bytes 98312 | tf_op jit(solution)/shard_map/ppermute | solution.py:474
  76.9 0.4 collective-permute-start.3
  77.4 1.4 %collective-permute-start.4 = (bf16[32,512]{1,0:T(8,128)(2,1)}, bf16[32,512]{1,0:T(8,128)(2,1)S(1)}, u32[]{:S(2)}, u32[]{:S(2)}) collective-permute-start(bf16[32,512]{1,0:T(8,128)(2,1)} %get-tuple-element.22), channel_id=1, source_target_pairs={{0,3},{1,2},{2,5},{3,4},{4,7},{5,6},{6,1},{7,0},{8,11},{9,10},{10,... | collective-permute-start | bytes 98312 | tf_op jit(solution)/shard_map/ppermute | solution.py:474
  78.8 0.0 collective-permute-done
  78.8 3.6 %collective-permute-start.5 = (bf16[32,512]{1,0:T(8,128)(2,1)}, bf16[32,512]{1,0:T(8,128)(2,1)S(1)}, u32[]{:S(2)}, u32[]{:S(2)}) collective-permute-start(bf16[32,512]{1,0:T(8,128)(2,1)} %get-tuple-element.23), channel_id=1, source_target_pairs={{0,7},{1,6},{2,1},{3,0},{4,3},{5,2},{6,5},{7,4},{8,15},{9,14},{10,... | collective-permute-start | bytes 98312 | tf_op jit(solution)/shard_map/ppermute | solution.py:474
  82.5 0.0 collective-permute-done.1
  82.5 1.7 %collective-permute-start.6 = (bf16[32,512]{1,0:T(8,128)(2,1)}, bf16[32,512]{1,0:T(8,128)(2,1)S(1)}, u32[]{:S(2)}, u32[]{:S(2)}) collective-permute-start(bf16[32,512]{1,0:T(8,128)(2,1)} %get-tuple-element.24), channel_id=1, source_target_pairs={{0,5},{1,4},{2,7},{3,6},{4,1},{5,0},{6,3},{7,2},{8,13},{9,12},{10,... | collective-permute-start | bytes 98312 | tf_op jit(solution)/shard_map/ppermute | solution.py:474
  84.2 0.0 copy-start
  84.2 6.7 %grads.1 = (bf16[3696,512]{1,0:T(8,128)(2,1)}, bf16[3696,512]{1,0:T(8,128)(2,1)}, bf16[3696,512]{1,0:T(8,128)(2,1)}) custom-call(bf16[3,3712,256]{2,1,0:T(8,128)(2,1)S(1)} %get-tuple-element.25.r, bf16[2,256,512]{2,1,0:T(8,128)(2,1)S(1)} %get-tuple-element.26.ab), custom_call_target="tpu_custom_call" | custom-call | flops 2906652672 | bytes 11354112 | tf_op jit(solution)/shard_map/grads/pallas_call | solution.py:451
  90.9 0.0 collective-permute-done.2
  90.9 0.0 collective-permute-done.3
  90.9 0.0 collective-permute-done.4
  90.9 0.0 collective-permute-done.5
  90.9 0.0 collective-permute-done.6
  90.9 0.0 copy-done
  90.9 0.7 convert_add_fusion
Async XLA Ops:
  71.9 6.9 %collective-permute-start = (bf16[32,512]{1,0:T(8,128)(2,1)}, bf16[32,512]{1,0:T(8,128)(2,1)S(1)}, u32[]{:S(2)}, u32[]{:S(2)}) collective-permute-start(bf16[32,512]{1,0:T(8,128)(2,1)} %get-tuple-element.18), channel_id=1, source_target_pairs={{0,2},{1,3},{2,4},{3,5},{4,6},{5,7},{6,0},{7,1},{8,10},{9,11},{10,... | collective-permute-start | bytes 98312 | tf_op jit(solution)/shard_map/ppermute | solution.py:474
  72.9 9.6 %collective-permute-start.1 = (bf16[32,512]{1,0:T(8,128)(2,1)}, bf16[32,512]{1,0:T(8,128)(2,1)S(1)}, u32[]{:S(2)}, u32[]{:S(2)}) collective-permute-start(bf16[32,512]{1,0:T(8,128)(2,1)} %get-tuple-element.19), channel_id=1, source_target_pairs={{0,6},{1,7},{2,0},{3,1},{4,2},{5,3},{6,4},{7,5},{8,14},{9,15},{10,... | collective-permute-start | bytes 98312 | tf_op jit(solution)/shard_map/ppermute | solution.py:474
  74.7 16.2 %collective-permute-start.2 = (bf16[32,512]{1,0:T(8,128)(2,1)}, bf16[32,512]{1,0:T(8,128)(2,1)S(1)}, u32[]{:S(2)}, u32[]{:S(2)}) collective-permute-start(bf16[32,512]{1,0:T(8,128)(2,1)} %get-tuple-element.20), channel_id=1, source_target_pairs={{0,1},{1,0},{2,3},{3,2},{4,5},{5,4},{6,7},{7,6},{8,9},{9,8},{10,11... | collective-permute-start | bytes 98312 | tf_op jit(solution)/shard_map/ppermute | solution.py:474
  76.9 13.9 %collective-permute-start.3 = (bf16[32,512]{1,0:T(8,128)(2,1)}, bf16[32,512]{1,0:T(8,128)(2,1)S(1)}, u32[]{:S(2)}, u32[]{:S(2)}) collective-permute-start(bf16[32,512]{1,0:T(8,128)(2,1)} %get-tuple-element.21), channel_id=1, source_target_pairs={{0,4},{1,5},{2,6},{3,7},{4,0},{5,1},{6,2},{7,3},{8,12},{9,13},{10,... | collective-permute-start | bytes 98312 | tf_op jit(solution)/shard_map/ppermute | solution.py:474
  77.4 13.5 %collective-permute-start.4 = (bf16[32,512]{1,0:T(8,128)(2,1)}, bf16[32,512]{1,0:T(8,128)(2,1)S(1)}, u32[]{:S(2)}, u32[]{:S(2)}) collective-permute-start(bf16[32,512]{1,0:T(8,128)(2,1)} %get-tuple-element.22), channel_id=1, source_target_pairs={{0,3},{1,2},{2,5},{3,4},{4,7},{5,6},{6,1},{7,0},{8,11},{9,10},{10,... | collective-permute-start | bytes 98312 | tf_op jit(solution)/shard_map/ppermute | solution.py:474
  78.8 12.1 %collective-permute-start.5 = (bf16[32,512]{1,0:T(8,128)(2,1)}, bf16[32,512]{1,0:T(8,128)(2,1)S(1)}, u32[]{:S(2)}, u32[]{:S(2)}) collective-permute-start(bf16[32,512]{1,0:T(8,128)(2,1)} %get-tuple-element.23), channel_id=1, source_target_pairs={{0,7},{1,6},{2,1},{3,0},{4,3},{5,2},{6,5},{7,4},{8,15},{9,14},{10,... | collective-permute-start | bytes 98312 | tf_op jit(solution)/shard_map/ppermute | solution.py:474
  82.5 8.4 %collective-permute-start.6 = (bf16[32,512]{1,0:T(8,128)(2,1)}, bf16[32,512]{1,0:T(8,128)(2,1)S(1)}, u32[]{:S(2)}, u32[]{:S(2)}) collective-permute-start(bf16[32,512]{1,0:T(8,128)(2,1)} %get-tuple-element.24), channel_id=1, source_target_pairs={{0,5},{1,4},{2,7},{3,6},{4,1},{5,0},{6,3},{7,2},{8,13},{9,12},{10,... | collective-permute-start | bytes 98312 | tf_op jit(solution)/shard_map/ppermute | solution.py:474
  84.2 6.7 %copy-start = (f32[32,512]{1,0:T(8,128)S(1)}, f32[32,512]{1,0:T(8,128)}, u32[]{:S(2)}) copy-start(f32[32,512]{1,0:T(8,128)} %get-tuple-element.17) | copy-start | bytes 196612

commit v5 on v3

--- a/solution.py
+++ b/solution.py
@@ -10,33 +10,56 @@
 BF16, F32 = jnp.bfloat16, jnp.float32
 MESH = pl.DeviceIdType.MESH
 LANE = 128
-TILES = (3, 3, 4, 4, 2, 5, 4, 4)
-REDUCE = ["zx", "zx", "xz", "zx", "xz", "zx", "zx", "xz"]
-GATHER = ["xz", "xz", "zx", "zx", "xz", "xz", "zx", "xz"]
+JOBS = (
+    ("E", 4, "xz", "zx"),
+    ("E", 5, "zx", "zx"),
+    ("L", 4, "zx", "xz"),
+    ("L", 5, "zx", "xz"),
+    ("T", 3, "zx", "xz"),
+    ("T", 1, "xz", "zx"),
+    ("T", 2, "zx", "zx"),
+    ("T", 3, "zx", "zx"),
+    ("T", 2, "zx", "xz"),
+)
 ORDER = (
-    (0, 0), (0, 1), (0, 2), (0, 3), (0, 4), (1, 0), (0, 5), (1, 1), (0, 6), (2, 0), (1, 2), (2, 1),
-    (1, 3), (1, 4), (0, 7), (3, 0), (1, 5), (3, 1), (1, 6), (2, 3), (2, 2), (1, 7), (2, 5), (4, 0),
-    (2, 4), (4, 1), (3, 3), (3, 2), (2, 6), (3, 5), (3, 4), (2, 7), (5, 0), (4, 2), (5, 1), (4, 3),
-    (3, 6), (4, 4), (4, 5), (3, 7), (6, 0), (5, 2), (4, 6), (5, 4), (6, 1), (5, 5), (5, 3), (4, 7),
-    (7, 0), (6, 2), (5, 6), (8, 0), (6, 4), (7, 1), (5, 7), (7, 2), (8, 1), (6, 5), (6, 3), (6, 6),
-    (7, 4), (8, 2), (7, 3), (6, 7), (8, 4), (7, 6), (7, 5), (8, 3), (7, 7), (8, 6), (8, 5), (8, 7),
+    (0, -1), (1, -1), (0, 0), (0, 1), (2, -1), (1, 0), (1, 1), (3, -1), (0, 2), (0, 3), (2, 1),
+    (2, 0), (1, 2), (1, 3), (0, 4), (0, 5), (0, 6), (3, 1), (3, 0), (1, 4), (2, 2), (2, 3), (4, 0),
+    (4, 1), (2, 4), (3, 2), (1, 5), (1, 6), (0, 7), (3, 3), (0, 8), (5, 0), (4, 2), (5, 1), (2, 5),
+    (1, 7), (1, 8), (4, 3), (6, 0), (3, 4), (2, 6), (6, 1), (3, 5), (2, 7), (5, 2), (2, 8), (3, 6),
+    (4, 5), (3, 7), (5, 3), (7, 0), (4, 4), (6, 2), (3, 8), (8, 0), (7, 1), (5, 5), (4, 6), (4, 7),
+    (6, 3), (5, 4), (4, 8), (8, 1), (7, 2), (6, 5), (5, 6), (5, 7), (5, 8), (7, 3), (8, 2), (7, 5),
+    (6, 4), (6, 6), (8, 3), (8, 5), (6, 7), (6, 8), (7, 6), (7, 4), (7, 8), (7, 7), (8, 6), (8, 4),
+    (8, 8), (8, 7),
 )
 NT = (((1,), (1,)), ((), ()))
 
 
-def chunks_of(width):
-    assert sum(TILES) == pl.cdiv(width, LANE)
-    out, at = [], 0
-    for t in TILES:
-        out.append((at * LANE, t * LANE, min(t * LANE, width - at * LANE)))
-        at += t
+def places_of(width):
+    out, at, pairs, taken = [], 0, 0, 0
+    for kind, tiles, _, _ in JOBS:
+        size = tiles * LANE
+        if kind == "E":
+            unit, pairs = pairs, pairs + 2 * size
+        elif kind == "L":
+            unit, taken = taken, taken + 2 * size
+        else:
+            assert taken == pairs or taken == 0
+            unit = max(pairs, units_end(out))
+        out.append((kind, at, unit, size, min(size, width - unit)))
+        at += 3 * size
+    assert taken == pairs and at == 3 * LANE * pl.cdiv(width, LANE)
     return out
 
 
+def units_end(places):
+    return max((unit + size for kind, _, unit, size, _ in places if kind == "T"), default=0)
+
+
 (
-    PAIR, ZA, ZB, ZUP, ZDOWN, X1, GUP, GDOWN, FUP, FDOWN, XA, XB, XC, XD, CA, CB, CC, CD,
-) = range(18)
-PER_CHUNK = 18
+    PAIR, PB, PC, PD, ZA, ZB, ZUP, ZDOWN, X1,
+    GUP, GDOWN, FUP, FDOWN, XA, XB, XC, XD, CA, CB, CC, CD,
+) = range(21)
+PER_CHUNK = 21
 COLS = 9 + 8
 
 
@@ -47,8 +70,10 @@
     wg, wu, wd, ab, pf, pr, zs1, zr1, zs2, zr2, own, xs, xr, res, rt, ig, igs, igr,
     ssem, rsem, lsem, osem,
 ):
-    chunks = chunks_of(width)
-    n = len(chunks)
+    places = places_of(width)
+    n = len(places)
+    cuts = [unit for kind, _, unit, _, _ in places if kind == "E"]
+    cuts += [max(unit + 2 * size for kind, _, unit, size, _ in places if kind == "E"), width]
     row, k = lax.axis_index("row"), lax.axis_index("col")
     x, z, c = row // 8, (row // 2) % 4, row % 2
     y, h = k // 2, k % 2
@@ -63,6 +88,9 @@
 
     sib, xn = rdev(x, z, 1 - c), rdev(1 - x, z, c)
     up, down = rdev(x, zp, c), rdev(x, zm, c)
+
+    def owner(slot):
+        return ((y, h), (ym, h), (yp, h), (y, 1 - h), (ym, 1 - h), (yp, 1 - h), (yo, h), (yo, 1 - h))[slot]
 
     sent = []
 
@@ -80,100 +108,125 @@
             device_id=sib, device_id_type=MESH,
         ).wait_recv()
 
-    mine = pl.ds(pl.multiple_of(k * 32, 32), 32)
     first = [
-        pltpu.make_async_copy(tok, ab.at[0, mine], lsem.at[0]),
-        pltpu.make_async_copy(og, ab.at[1, mine], lsem.at[1]),
+        pltpu.make_async_copy(tok, ab.at[0, :32], lsem.at[0]),
+        pltpu.make_async_copy(og, ab.at[1, :32], lsem.at[1]),
     ]
     weights = [
-        pltpu.make_async_copy(wg_h, wg, lsem.at[2]),
-        pltpu.make_async_copy(wu_h, wu, lsem.at[3]),
-        pltpu.make_async_copy(wd_h, wd, lsem.at[4]),
+        [
+            pltpu.make_async_copy(src.at[rows], dst.at[rows], lsem.at[2 + 3 * i + w])
+            for w, (src, dst) in enumerate(((wg_h, wg), (wu_h, wu), (wd_h, wd)))
+        ]
+        for i, rows in enumerate(pl.ds(a, b - a) for a, b in zip(cuts, cuts[1:]))
     ]
-    for copy in first + weights:
+    for copy in first + sum(weights, []):
         copy.start()
 
     barrier = pltpu.get_barrier_semaphore()
     greeted = [sib, xn, up, down]
-    for step in range(1, 8):
-        greeted.append((row, (k + step) % 8))
+    for slot in range(1, 8):
+        greeted.append(cdev(*owner(slot)))
     for dev in greeted:
         pl.semaphore_signal(barrier, inc=1, device_id=dev, device_id_type=MESH)
+    ig[...] = jnp.zeros_like(ig)
     for copy in first:
         copy.wait()
     pl.semaphore_wait(barrier, len(greeted))
 
     base = n * PER_CHUNK
 
-    def block(yy, hh):
-        return pl.ds(pl.multiple_of((yy * 2 + hh) * 32, 32), 32)
-
-    def both(yy, hh):
-        return ab.at[:, block(yy, hh)]
-
-    def one(part, yy, hh):
-        return ab.at[part, block(yy, hh)]
-
-    me = both(y, h)
-    send(me, me, base + 2, cdev(y, 1 - h))
-    send(me, me, base + 0, cdev(yp, h))
-    send(me, me, base + 1, cdev(ym, h))
-    landed(both(ym, h), base + 0)
-    send(one(0, ym, h), one(0, ym, h), base + 5, cdev(yp, h))
-    landed(both(yp, h), base + 1)
-    send(one(1, yp, h), one(1, yp, h), base + 6, cdev(ym, h))
-    landed(both(y, 1 - h), base + 2)
-    send(both(y, 1 - h), both(y, 1 - h), base + 3, cdev(yp, h))
-    send(both(y, 1 - h), both(y, 1 - h), base + 4, cdev(ym, h))
-    landed(both(ym, 1 - h), base + 3)
-    send(one(0, ym, 1 - h), one(0, ym, 1 - h), base + 7, cdev(yp, h))
-    landed(both(yp, 1 - h), base + 4)
-    send(one(1, yp, 1 - h), one(1, yp, 1 - h), base + 8, cdev(ym, h))
-    landed(one(0, yo, h), base + 5)
-    landed(one(1, yo, h), base + 6)
-    landed(one(0, yo, 1 - h), base + 7)
-    landed(one(1, yo, 1 - h), base + 8)
-    outs = [pltpu.make_async_copy(ab, ab_out, osem.at[0])]
-    outs[0].start()
-    for copy in weights:
-        copy.wait()
-
-    first_token = c * 128 + x * 64 + z * 16
-    lanes = lax.broadcasted_iota(jnp.int32, (16, 256), 1)
-    rows = lax.broadcasted_iota(jnp.int32, (16, 256), 0)
-    column = jnp.sum(
-        jnp.where(lanes == rows + first_token, jnp.broadcast_to(tw[...], (16, 256)), 0.0),
-        axis=1, keepdims=True,
-    )
+    def both(slot):
+        return ab.at[:, slot * 32 : slot * 32 + 32]
+
+    def one(part, slot):
+        return ab.at[part, slot * 32 : slot * 32 + 32]
+
+    send(both(0), both(3), base + 2, cdev(y, 1 - h))
+    send(both(0), both(1), base + 0, cdev(yp, h))
+    send(both(0), both(2), base + 1, cdev(ym, h))
+
+    def col_near():
+        landed(both(1), base + 0)
+        send(one(0, 1), one(0, 6), base + 5, cdev(yp, h))
+        landed(both(2), base + 1)
+        send(one(1, 2), one(1, 6), base + 6, cdev(ym, h))
+
+    def col_cross():
+        landed(both(3), base + 2)
+        send(both(3), both(4), base + 3, cdev(yp, h))
+        send(both(3), both(5), base + 4, cdev(ym, h))
+
+    def col_next():
+        landed(both(4), base + 3)
+        send(one(0, 4), one(0, 7), base + 7, cdev(yp, h))
+        landed(both(5), base + 4)
+        send(one(1, 5), one(1, 7), base + 8, cdev(ym, h))
+
+    outs = []
+
+    def col_far():
+        landed(one(0, 6), base + 5)
+        landed(one(1, 6), base + 6)
+        landed(one(0, 7), base + 7)
+        landed(one(1, 7), base + 8)
+        copy = pltpu.make_async_copy(ab, ab_out, osem.at[0])
+        copy.start()
+        outs.append(copy)
+
+    def column_of(half):
+        lanes = lax.broadcasted_iota(jnp.int32, (16, 256), 1)
+        rows = lax.broadcasted_iota(jnp.int32, (16, 256), 0)
+        place, among = x * 2 + z // 2, 0
+        for i in range(4):
+            yy, hh = owner(4 * half + i)
+            among = among + jnp.where(place == i, (yy * 2 + hh) * 32, 0)
+        at = rows + (among + (z % 2) * 16)
+        return jnp.sum(
+            jnp.where(lanes == at, jnp.broadcast_to(tw[...], (16, 256)), 0.0), axis=1, keepdims=True
+        )
+
+    columns = {"E": column_of(0), "L": column_of(1)}
+    columns["T"] = jnp.where(c == 0, columns["E"], columns["L"])
 
     def span(j):
-        o, w, _ = chunks[j]
-        return slice(3 * o, 3 * o + 3 * w)
+        _, at, _, size, _ = places[j]
+        return slice(at, at + 3 * size)
 
     def halves(j):
-        o, w, _ = chunks[j]
-        cut = 3 * o + (3 * w // LANE // 2) * LANE
-        return slice(3 * o, cut), slice(cut, 3 * o + 3 * w)
+        _, at, _, size, _ = places[j]
+        cut = at + (3 * size // LANE // 2) * LANE
+        return slice(at, cut), slice(cut, at + 3 * size)
 
     def products(j):
-        o, w, valid = chunks[j]
+        kind, base_at, unit, size, valid = places[j]
+        m, cols = j * PER_CHUNK, span(j)
+        for group in weights[: j + 1 if kind == "E" else None]:
+            while group:
+                group.pop(0).wait()
+        rows = {"E": slice(0, 128), "L": slice(128, 256), "T": slice(0, 256)}[kind]
         for part in range(3):
-            for at in range(0, valid, 256):
-                size = min(256, valid - at)
-                lo = o + at
-                value = lax.dot_general(
-                    ab[part // 2], (wg, wu, wd)[part][lo : lo + size, :], NT,
-                    preferred_element_type=F32,
-                )
-                to = 3 * o + part * w + at
-                pf[:, :, :, :, to : to + size] = value.reshape(2, 2, 4, 16, size)
-            if valid < w:
-                pad = slice(3 * o + part * w + valid, 3 * o + part * w + w)
-                pf[:, :, :, :, pad] = jnp.zeros((2, 2, 4, 16, w - valid), F32)
-        cols = span(j)
-        send(
-            pf.at[1 - c, :, :, :, cols], pr.at[:, :, :, cols], j * PER_CHUNK + PAIR, sib
-        )
+            side, wide = ab.at[part // 2], (wg, wu, wd)[part]
+            for half in range(1 if kind == "T" else 2):
+                for at in range(0, valid, 256):
+                    span_ = min(256, valid - at)
+                    lo = unit + half * size + at
+                    value = lax.dot_general(
+                        side[rows, :], wide[lo : lo + span_, :], NT, preferred_element_type=F32
+                    )
+                    to = base_at + part * size + at
+                    if kind == "T":
+                        pf[:, :, :, :, to : to + span_] = value.reshape(2, 2, 4, 16, span_)
+                    else:
+                        pf[half, :, :, :, to : to + span_] = value.reshape(2, 4, 16, span_)
+            if valid < size:
+                pad = slice(base_at + part * size + valid, base_at + part * size + size)
+                pf[:, :, :, :, pad] = jnp.zeros((2, 2, 4, 16, size - valid), F32)
+        if JOBS[j][2] == "zx":
+            for zz, idx in ((zo, PAIR), (zp, PB), (zm, PC), (z, PD)):
+                send(pf.at[1 - c, :, zz, :, cols], pr.at[:, zz, :, cols], m + idx, sib)
+        else:
+            for xx, idx in ((1 - x, PAIR), (x, PB)):
+                send(pf.at[1 - c, xx, :, :, cols], pr.at[xx, :, :, cols], m + idx, sib)
 
     def chip(xx, zz, cols):
         return pf[c, xx, zz, :, cols] + pr[xx, zz, :, cols]
@@ -183,7 +236,7 @@
 
     def zx_far(j):
         m, cols = j * PER_CHUNK, span(j)
-        landed(pr.at[:, :, :, cols], m + PAIR)
+        landed(pr.at[:, zo, :, cols], m + PAIR)
         zs1[0, :, cols] = chip(0, zo, cols).astype(BF16)
         send(zs1.at[0, :, cols], zr1.at[0, :, cols], m + ZA, up)
         zs1[1, :, cols] = chip(1, zo, cols).astype(BF16)
@@ -191,10 +244,12 @@
 
     def zx_near(j):
         m, cols = j * PER_CHUNK, span(j)
+        landed(pr.at[:, zp, :, cols], m + PB)
         landed(zr1.at[0, :, cols], m + ZA)
         zs2[0, 0, :, cols] = (chip(0, zp, cols) + zr1[0, :, cols].astype(F32)).astype(BF16)
         zs2[0, 1, :, cols] = chip(1, zp, cols).astype(BF16)
         send(zs2.at[0, :, :, cols], zr2.at[0, :, :, cols], m + ZUP, up)
+        landed(pr.at[:, zm, :, cols], m + PC)
         landed(zr1.at[1, :, cols], m + ZB)
         zs2[1, 0, :, cols] = chip(0, zm, cols).astype(BF16)
         zs2[1, 1, :, cols] = (chip(1, zm, cols) + zr1[1, :, cols].astype(F32)).astype(BF16)
@@ -202,6 +257,7 @@
 
     def zx_cross(j):
         m, cols = j * PER_CHUNK, span(j)
+        landed(pr.at[:, z, :, cols], m + PD)
         landed(zr2.at[0, :, :, cols], m + ZUP)
         landed(zr2.at[1, :, :, cols], m + ZDOWN)
 
@@ -219,13 +275,14 @@
 
     def xz_cross(j):
         m, cols = j * PER_CHUNK, span(j)
-        landed(pr.at[:, :, :, cols], m + PAIR)
+        landed(pr.at[1 - x, :, :, cols], m + PAIR)
         xs[:, :, cols] = (pf[c, 1 - x, :, :, cols] + pr[1 - x, :, :, cols]).astype(BF16)
         send(xs.at[:, :, cols], xr.at[:, :, cols], m + X1, xn)
 
     def xz_far(j):
         m, cols = j * PER_CHUNK, span(j)
         lo, hi = halves(j)
+        landed(pr.at[x, :, :, cols], m + PB)
         landed(xr.at[:, :, cols], m + X1)
         zs1[0, :, lo] = chip_sum(x, zo, lo).astype(BF16)
         send(zs1.at[0, :, lo], zr1.at[0, :, lo], m + ZA, up)
@@ -263,12 +320,13 @@
         send(part, part, idx, dev)
 
     def activate(j):
-        o, w, _ = chunks[j]
-        m, cols = j * PER_CHUNK, span(j)
-        total = (xz_total if REDUCE[j] == "xz" else zx_total)(j)
+        kind, base_at, _, size, _ = places[j]
+        m, cols = j * PER_CHUNK, span(j)
+        total = (xz_total if JOBS[j][2] == "xz" else zx_total)(j)
+        column = columns[kind]
 
         def place(part):
-            return slice(3 * o + part * w, 3 * o + part * w + w)
+            return slice(base_at + part * size, base_at + part * size + size)
 
         gate, linear, back = total(place(0)), total(place(1)), total(place(2))
         sig = jax.nn.sigmoid(gate)
@@ -281,7 +339,7 @@
         )):
             res[c, x, z, :, place(part)] = value.astype(BF16)
         push(x, z, cols, m + XA, xn)
-        if GATHER[j] == "zx":
+        if JOBS[j][3] == "zx":
             push(x, z, cols, m + GUP, up)
             push(x, z, cols, m + GDOWN, down)
 
@@ -346,22 +404,33 @@
             landed(res.at[1 - c, :, zz, :, cols], m + idx)
 
     def finish(j):
-        o, w, valid = chunks[j]
-        m, cols = j * PER_CHUNK, span(j)
-        (zx_all if GATHER[j] == "zx" else xz_all)(j)
-        for part, wide in ((1, wg), (2, wu)):
-            at = 3 * o + part * w
-            piece = res[:, :, :, :, at : at + valid].reshape(256, valid)
-            value = jnp.dot(piece, wide[o : o + valid, :], preferred_element_type=F32)
-            if j == 0 and part == 1:
-                ig[...] = value
-            else:
-                ig[...] += value
-        for part in range(3):
-            at = 3 * o + part * w
-            rt[part, o : o + w, :] = res[:, :, :, :, at : at + w].reshape(256, w).T
+        kind, base_at, unit, size, valid = places[j]
+        (zx_all if JOBS[j][3] == "zx" else xz_all)(j)
+        if kind == "T":
+            pieces = [(slice(0, 256), unit, lambda at: res[:, :, :, :, at].reshape(256, -1))]
+            tokens, units = pl.ds(0, 256), pl.ds(unit, size)
+        else:
+            start = 128 * (kind == "L")
+            pieces = [
+                (
+                    slice(start, start + 128), unit + half * size,
+                    lambda at, half=half: res[half, :, :, :, at].reshape(128, -1),
+                )
+                for half in range(2)
+            ]
+            tokens, units = pl.ds(start, 128), pl.ds(unit, 2 * size)
+        for rows, lo, piece in pieces:
+            for part, wide in ((1, wg), (2, wu)):
+                at = base_at + part * size
+                ig[rows, :] += jnp.dot(
+                    piece(slice(at, at + valid)), wide[lo : lo + valid, :],
+                    preferred_element_type=F32,
+                )
+            for part in range(3):
+                at = base_at + part * size
+                rt[part, lo : lo + size, rows] = piece(slice(at, at + size)).T
         copy = pltpu.make_async_copy(
-            rt.at[:, o : o + w], r_out.at[:, o : o + w], osem.at[1 + j]
+            rt.at[:, units, tokens], r_out.at[:, units, tokens], osem.at[1 + j]
         )
         copy.start()
         outs.append(copy)
@@ -371,20 +440,23 @@
         "zx": (zx_gather_near, zx_gather_far, zx_gather_cross),
         "xz": (xz_gather_cross, xz_gather_near, xz_gather_far),
     }
+    col = (col_near, col_cross, col_next, col_far)
     for stage, j in ORDER:
-        (products, *reduce[REDUCE[j]], activate, *gather[GATHER[j]], finish)[stage](j)
+        if j < 0:
+            col[stage]()
+        else:
+            _, _, over, back = JOBS[j]
+            (products, *reduce[over], activate, *gather[back], finish)[stage](j)
 
     igs[...] = ig[...].astype(BF16)
-    for step in range(1, 8):
-        other = (k + step) % 8
+    for slot in range(1, 8):
         send(
-            igs.at[pl.ds(pl.multiple_of(other * 32, 32), 32)], igr.at[step], base + 9 + step,
-            (row, other),
+            igs.at[slot * 32 : slot * 32 + 32], igr.at[slot], base + 9 + slot, cdev(*owner(slot))
         )
-    total = ig[mine, :]
-    for step in range(1, 8):
-        landed(igr.at[step], base + 9 + step)
-        total = total + igr[step].astype(F32)
+    total = ig[:32, :]
+    for slot in range(1, 8):
+        landed(igr.at[slot], base + 9 + slot)
+        total = total + igr[slot].astype(F32)
     ig_out[...] = total
 
     for copy in sent:
@@ -397,7 +469,7 @@
     width, depth = gate_weight.shape
     wide = pl.cdiv(width, LANE) * LANE
     cols = 3 * wide
-    n = len(TILES)
+    n = len(JOBS)
     messages = n * PER_CHUNK + COLS
     hbm = pl.BlockSpec(memory_space=pl.ANY)
     vmem = pl.BlockSpec(memory_space=pltpu.VMEM)
@@ -431,7 +503,7 @@
             pltpu.VMEM((8, 32, depth), BF16),
             pltpu.SemaphoreType.DMA((messages,)),
             pltpu.SemaphoreType.DMA((messages,)),
-            pltpu.SemaphoreType.DMA((5,)),
+            pltpu.SemaphoreType.DMA((2 + 3 * n,)),
             pltpu.SemaphoreType.DMA((1 + n,)),
         ],
         compiler_params=pltpu.CompilerParams(

time: 86.4 us -> 86.6 us (level)
  no operation moved by 1% of the time
where the time goes in v5:
time: 86.6 us; the launch traced here: 86.5 us
  Pallas kernels  85.2 us (98%)
    pallas_call x1, Pallas kernels, exchange(): pl.pallas_call(functools.partial(exchange_kernel, width), out_shape=(pltp...  78.5 us
    pallas_call x1, Pallas kernels, grads(): pl.pallas_call(grads_kernel, grid=(pl.cdiv(width, step),), in_specs=[pl.B...  6.68 us

profile of v5, /device:TPU:1, one launch (start us, length us, event | category | flops | bytes accessed | tf_op | source)
XLA Modules:
  0.0 86.5 jit_solution(13501688357883773628)
XLA Ops:
  0.6 78.5 %exchange.1 = (bf16[3,3712,256]{2,1,0:T(8,128)(2,1)S(1)}, bf16[2,256,512]{2,1,0:T(8,128)(2,1)S(1)}, f32[32,512]{1,0:T(8,128)}) custom-call(bf16[32,512]{1,0:T(8,128)(2,1)} %tok.1, bf16[32,512]{1,0:T(8,128)(2,1)} %og.1, f32[1,256]{1,0:T(1,128)} %bitcast.9, bf16[3696,512]{1,0:T(8,128)(2,1)} %bitcast.5, bf16[3696,512]{1,0:T(8,128)(2,1)} %bitcast.6, ...), custom_call_target="tpu_custom_call" | custom-call | flops 4844421120 | bytes 17031168 | tf_op jit(solution)/shard_map/exchange/pallas_call | solution.py:476
  79.1 0.0 copy-start
  79.2 6.7 %grads.1 = (bf16[3696,512]{1,0:T(8,128)(2,1)}, bf16[3696,512]{1,0:T(8,128)(2,1)}, bf16[3696,512]{1,0:T(8,128)(2,1)}) custom-call(bf16[3,3712,256]{2,1,0:T(8,128)(2,1)S(1)} %get-tuple-element.11.r, bf16[2,256,512]{2,1,0:T(8,128)(2,1)S(1)} %get-tuple-element.12.ab), custom_call_target="tpu_custom_call" | custom-call | tf_op jit(solution)/shard_map/grads/pallas_call | solution.py:531
  85.8 0.0 copy-done
  85.8 0.6 copy.11
Async XLA Ops:
  79.1 6.7 %copy-start = (f32[32,512]{1,0:T(8,128)S(1)}, f32[32,512]{1,0:T(8,128)}, u32[]{:S(2)}) copy-start(f32[32,512]{1,0:T(8,128)} %get-tuple-element.20) | copy-start | bytes 196612

commit v6 on v5

--- a/solution.py
+++ b/solution.py
@@ -11,25 +11,26 @@
 MESH = pl.DeviceIdType.MESH
 LANE = 128
 JOBS = (
-    ("E", 4, "xz", "zx"),
-    ("E", 5, "zx", "zx"),
-    ("L", 4, "zx", "xz"),
-    ("L", 5, "zx", "xz"),
+    ("E", 4, "zx", "zx"),
+    ("L", 4, "xz", "zx"),
+    ("T", 4, "zx", "xz"),
     ("T", 3, "zx", "xz"),
-    ("T", 1, "xz", "zx"),
+    ("T", 4, "xz", "zx"),
+    ("T", 3, "zx", "xz"),
+    ("T", 3, "zx", "xz"),
+    ("T", 2, "xz", "zx"),
     ("T", 2, "zx", "zx"),
-    ("T", 3, "zx", "zx"),
-    ("T", 2, "zx", "xz"),
 )
 ORDER = (
-    (0, -1), (1, -1), (0, 0), (0, 1), (2, -1), (1, 0), (1, 1), (3, -1), (0, 2), (0, 3), (2, 1),
-    (2, 0), (1, 2), (1, 3), (0, 4), (0, 5), (0, 6), (3, 1), (3, 0), (1, 4), (2, 2), (2, 3), (4, 0),
-    (4, 1), (2, 4), (3, 2), (1, 5), (1, 6), (0, 7), (3, 3), (0, 8), (5, 0), (4, 2), (5, 1), (2, 5),
-    (1, 7), (1, 8), (4, 3), (6, 0), (3, 4), (2, 6), (6, 1), (3, 5), (2, 7), (5, 2), (2, 8), (3, 6),
-    (4, 5), (3, 7), (5, 3), (7, 0), (4, 4), (6, 2), (3, 8), (8, 0), (7, 1), (5, 5), (4, 6), (4, 7),
-    (6, 3), (5, 4), (4, 8), (8, 1), (7, 2), (6, 5), (5, 6), (5, 7), (5, 8), (7, 3), (8, 2), (7, 5),
-    (6, 4), (6, 6), (8, 3), (8, 5), (6, 7), (6, 8), (7, 6), (7, 4), (7, 8), (7, 7), (8, 6), (8, 4),
-    (8, 8), (8, 7),
+    (0, -1), (1, -1), (0, 0), (1, 0), (2, -1), (2, 0), (3, -1), (0, 1), (1, 1), (3, 0), (0, 2),
+    (1, 2), (0, 3), (1, 3), (2, 1), (0, 4), (2, 2), (4, 0), (1, 4), (0, 5), (2, 3), (1, 5), (0, 6),
+    (3, 2), (2, 4), (1, 6), (3, 1), (3, 3), (5, 0), (2, 5), (0, 7), (2, 6), (1, 7), (4, 2), (0, 8),
+    (4, 1), (1, 8), (4, 3), (2, 7), (3, 4), (6, 0), (2, 8), (3, 5), (5, 2), (3, 6), (5, 1), (5, 3),
+    (7, 0), (4, 4), (3, 8), (3, 7), (4, 5), (4, 6), (6, 2), (6, 1), (6, 3), (5, 4), (8, 0), (4, 7),
+    (4, 8), (5, 5), (5, 6), (7, 2), (9, 0), (7, 1), (10, 0), (7, 3), (6, 4), (5, 8), (6, 5), (5, 7),
+    (8, 2), (6, 6), (8, 1), (8, 3), (7, 4), (6, 8), (9, 2), (10, 2), (7, 5), (9, 1), (9, 3), (6, 7),
+    (10, 1), (8, 4), (7, 6), (7, 8), (10, 3), (8, 5), (7, 7), (9, 4), (8, 6), (8, 8), (10, 4),
+    (9, 5), (10, 5), (8, 7), (9, 6), (9, 8), (10, 6), (10, 8), (9, 7), (4, -1), (10, 7),
 )
 NT = (((1,), (1,)), ((), ()))
 
@@ -67,13 +68,11 @@
     width,
     tok, og, tw, wg_h, wu_h, wd_h,
     r_out, ab_out, ig_out,
-    wg, wu, wd, ab, pf, pr, zs1, zr1, zs2, zr2, own, xs, xr, res, rt, ig, igs, igr,
+    wgu, wd, ab, pf, pr, zs1, zr1, zs2, zr2, own, xs, xr, res, rt, ig, igs, igr,
     ssem, rsem, lsem, osem,
 ):
     places = places_of(width)
     n = len(places)
-    cuts = [unit for kind, _, unit, _, _ in places if kind == "E"]
-    cuts += [max(unit + 2 * size for kind, _, unit, size, _ in places if kind == "E"), width]
     row, k = lax.axis_index("row"), lax.axis_index("col")
     x, z, c = row // 8, (row // 2) % 4, row % 2
     y, h = k // 2, k % 2
@@ -112,13 +111,20 @@
         pltpu.make_async_copy(tok, ab.at[0, :32], lsem.at[0]),
         pltpu.make_async_copy(og, ab.at[1, :32], lsem.at[1]),
     ]
-    weights = [
-        [
-            pltpu.make_async_copy(src.at[rows], dst.at[rows], lsem.at[2 + 3 * i + w])
-            for w, (src, dst) in enumerate(((wg_h, wg), (wu_h, wu), (wd_h, wd)))
-        ]
-        for i, rows in enumerate(pl.ds(a, b - a) for a, b in zip(cuts, cuts[1:]))
-    ]
+    weights = [[] for _ in places]
+    for j, (kind, _, unit, size, valid) in enumerate(places):
+        if kind == "L":
+            continue
+        for lo in (unit,) if kind == "T" else (unit, unit + size):
+            for src, dst, to in (
+                (wg_h, wgu, 2 * lo), (wu_h, wgu, 2 * lo + size), (wd_h, wd, lo)
+            ):
+                weights[j].append(pltpu.make_async_copy(
+                    src.at[pl.ds(lo, valid)], dst.at[pl.ds(to, valid)],
+                    lsem.at[2 + 6 * j + len(weights[j])],
+                ))
+                if valid < size:
+                    dst[to + valid : to + size, :] = jnp.zeros((size - valid, dst.shape[1]), BF16)
     for copy in first + sum(weights, []):
         copy.start()
 
@@ -197,30 +203,39 @@
         cut = at + (3 * size // LANE // 2) * LANE
         return slice(at, cut), slice(cut, at + 3 * size)
 
+    def multiply(j, side, wide, first, count, to):
+        kind, _, unit, size, _ = places[j]
+        rows = {"E": slice(0, 128), "L": slice(128, 256), "T": slice(0, 256)}[kind]
+
+        def block(half, lo, at, width):
+            value = lax.dot_general(
+                ab[side, rows, :], wide[pl.ds(lo, width), :], NT, preferred_element_type=F32
+            )
+            if kind == "T":
+                pf[:, :, :, :, pl.ds(at, width)] = value.reshape(2, 2, 4, 16, width)
+            else:
+                pf[half, :, :, :, pl.ds(at, width)] = value.reshape(2, 4, 16, width)
+
+        for half in range(1 if kind == "T" else 2):
+            lo = first + half * count
+
+            @pl.loop(0, count // 256)
+            def _(i):
+                block(half, pl.multiple_of(lo + i * 256, 128), pl.multiple_of(to + i * 256, 128), 256)
+
+            if count % 256:
+                block(half, lo + count - 128, to + count - 128, 128)
+
     def products(j):
-        kind, base_at, unit, size, valid = places[j]
-        m, cols = j * PER_CHUNK, span(j)
-        for group in weights[: j + 1 if kind == "E" else None]:
-            while group:
-                group.pop(0).wait()
-        rows = {"E": slice(0, 128), "L": slice(128, 256), "T": slice(0, 256)}[kind]
-        for part in range(3):
-            side, wide = ab.at[part // 2], (wg, wu, wd)[part]
-            for half in range(1 if kind == "T" else 2):
-                for at in range(0, valid, 256):
-                    span_ = min(256, valid - at)
-                    lo = unit + half * size + at
-                    value = lax.dot_general(
-                        side[rows, :], wide[lo : lo + span_, :], NT, preferred_element_type=F32
-                    )
-                    to = base_at + part * size + at
-                    if kind == "T":
-                        pf[:, :, :, :, to : to + span_] = value.reshape(2, 2, 4, 16, span_)
-                    else:
-                        pf[half, :, :, :, to : to + span_] = value.reshape(2, 4, 16, span_)
-            if valid < size:
-                pad = slice(base_at + part * size + valid, base_at + part * size + size)
-                pf[:, :, :, :, pad] = jnp.zeros((2, 2, 4, 16, size - valid), F32)
+        kind, base_at, unit, size, _ = places[j]
+        for copy in weights[j]:
+            copy.wait()
+        multiply(j, 0, wgu, 2 * unit, 2 * size, base_at)
+
+    def back_products(j):
+        _, base_at, unit, size, _ = places[j]
+        m, cols = j * PER_CHUNK, span(j)
+        multiply(j, 1, wd, unit, size, base_at + 2 * size)
         if JOBS[j][2] == "zx":
             for zz, idx in ((zo, PAIR), (zp, PB), (zm, PC), (z, PD)):
                 send(pf.at[1 - c, :, zz, :, cols], pr.at[:, zz, :, cols], m + idx, sib)
@@ -333,9 +348,9 @@
         silu = gate * sig
         scaled = column * back
         for part, value in enumerate((
-            column * (silu * linear),
             scaled * linear * sig * (1.0 + gate * (1.0 - sig)),
             scaled * silu,
+            column * (silu * linear),
         )):
             res[c, x, z, :, place(part)] = value.astype(BF16)
         push(x, z, cols, m + XA, xn)
@@ -404,55 +419,80 @@
             landed(res.at[1 - c, :, zz, :, cols], m + idx)
 
     def finish(j):
-        kind, base_at, unit, size, valid = places[j]
+        kind, base_at, unit, size, _ = places[j]
         (zx_all if JOBS[j][3] == "zx" else xz_all)(j)
+        at = slice(base_at, base_at + 2 * size)
         if kind == "T":
-            pieces = [(slice(0, 256), unit, lambda at: res[:, :, :, :, at].reshape(256, -1))]
+            piece = res[:, :, :, :, at].reshape(256, 2 * size)
+            ig[...] += jnp.dot(
+                piece, wgu[2 * unit : 2 * unit + 2 * size, :], preferred_element_type=F32
+            )
+        else:
+            start = 128 * (kind == "L")
+            lo = 2 * unit
+            value = jnp.dot(
+                res[0, :, :, :, at].reshape(128, 2 * size), wgu[lo : lo + 2 * size, :],
+                preferred_element_type=F32,
+            )
+            lo += 2 * size
+            value += jnp.dot(
+                res[1, :, :, :, at].reshape(128, 2 * size), wgu[lo : lo + 2 * size, :],
+                preferred_element_type=F32,
+            )
+            ig[start : start + 128, :] += value
+
+    def transposes(j):
+        kind, base_at, unit, size, _ = places[j]
+        for part in range(3):
+            at = base_at + part * size
+
+            @pl.loop(0, size // LANE)
+            def _(i):
+                cols = pl.ds(pl.multiple_of(at + i * LANE, LANE), LANE)
+                if kind == "T":
+                    to = pl.ds(pl.multiple_of(unit + i * LANE, LANE), LANE)
+                    rt[part, to, :] = res[:, :, :, :, cols].reshape(256, LANE).T
+                else:
+                    start = 128 * (kind == "L")
+                    for half in range(2):
+                        to = pl.ds(pl.multiple_of(unit + half * size + i * LANE, LANE), LANE)
+                        rt[part, to, start : start + 128] = (
+                            res[half, :, :, :, cols].reshape(128, LANE).T
+                        )
+
+        if kind == "T":
             tokens, units = pl.ds(0, 256), pl.ds(unit, size)
         else:
-            start = 128 * (kind == "L")
-            pieces = [
-                (
-                    slice(start, start + 128), unit + half * size,
-                    lambda at, half=half: res[half, :, :, :, at].reshape(128, -1),
-                )
-                for half in range(2)
-            ]
-            tokens, units = pl.ds(start, 128), pl.ds(unit, 2 * size)
-        for rows, lo, piece in pieces:
-            for part, wide in ((1, wg), (2, wu)):
-                at = base_at + part * size
-                ig[rows, :] += jnp.dot(
-                    piece(slice(at, at + valid)), wide[lo : lo + valid, :],
-                    preferred_element_type=F32,
-                )
-            for part in range(3):
-                at = base_at + part * size
-                rt[part, lo : lo + size, rows] = piece(slice(at, at + size)).T
+            tokens, units = pl.ds(128 * (kind == "L"), 128), pl.ds(unit, 2 * size)
         copy = pltpu.make_async_copy(
             rt.at[:, units, tokens], r_out.at[:, units, tokens], osem.at[1 + j]
         )
         copy.start()
         outs.append(copy)
 
+    def col_send():
+        igs[...] = ig[...].astype(BF16)
+        for slot in range(1, 8):
+            send(
+                igs.at[slot * 32 : slot * 32 + 32], igr.at[slot], base + 9 + slot,
+                cdev(*owner(slot)),
+            )
+
     reduce = {"zx": (zx_far, zx_near, zx_cross), "xz": (xz_cross, xz_far, xz_near)}
     gather = {
         "zx": (zx_gather_near, zx_gather_far, zx_gather_cross),
         "xz": (xz_gather_cross, xz_gather_near, xz_gather_far),
     }
-    col = (col_near, col_cross, col_next, col_far)
+    col = (col_near, col_cross, col_next, col_far, col_send)
     for stage, j in ORDER:
         if j < 0:
             col[stage]()
         else:
             _, _, over, back = JOBS[j]
-            (products, *reduce[over], activate, *gather[back], finish)[stage](j)
-
-    igs[...] = ig[...].astype(BF16)
-    for slot in range(1, 8):
-        send(
-            igs.at[slot * 32 : slot * 32 + 32], igr.at[slot], base + 9 + slot, cdev(*owner(slot))
-        )
+            (
+                products, back_products, *reduce[over], activate, *gather[back], finish, transposes,
+            )[stage](j)
+
     total = ig[:32, :]
     for slot in range(1, 8):
         landed(igr.at[slot], base + 9 + slot)
@@ -483,9 +523,8 @@
         in_specs=[hbm, hbm, vmem, hbm, hbm, hbm],
         out_specs=(hbm, hbm, vmem),
         scratch_shapes=[
-            pltpu.VMEM((width, depth), BF16),
-            pltpu.VMEM((width, depth), BF16),
-            pltpu.VMEM((width, depth), BF16),
+            pltpu.VMEM((2 * wide, depth), BF16),
+            pltpu.VMEM((wide, depth), BF16),
             pltpu.VMEM((2, 256, depth), BF16),
             pltpu.VMEM((2, 2, 4, 16, cols), F32),
             pltpu.VMEM((2, 4, 16, cols), F32),
@@ -503,7 +542,7 @@
             pltpu.VMEM((8, 32, depth), BF16),
             pltpu.SemaphoreType.DMA((messages,)),
             pltpu.SemaphoreType.DMA((messages,)),
-            pltpu.SemaphoreType.DMA((2 + 3 * n,)),
+            pltpu.SemaphoreType.DMA((2 + 6 * n,)),
             pltpu.SemaphoreType.DMA((1 + n,)),
         ],
         compiler_params=pltpu.CompilerParams(
@@ -517,27 +556,61 @@
     )(tokens, out_grad, token_weight.reshape(1, 256), gate_weight, up_weight, down_weight)
 
 
-def grads_kernel(r, ab, gate_grad, up_grad, down_grad):
-    for part, out in ((1, gate_grad), (2, up_grad), (0, down_grad)):
-        out[...] = jnp.dot(
-            r[part], ab[0 if part else 1], preferred_element_type=F32
-        ).astype(BF16)
+GRAD_ROWS = 336
+
+
+def grads_kernel(r_h, ab_h, gate_grad, up_grad, down_grad, r, ab, out, isem, osem):
+    step = GRAD_ROWS
+    n = gate_grad.shape[0] // step
+
+    def load(i):
+        rows = pl.ds(pl.multiple_of(i * step, 16), step)
+        return pltpu.make_async_copy(r_h.at[:, rows], r.at[:, rows], isem.at[i])
+
+    def store(i, part):
+        rows = pl.ds(pl.multiple_of(i * step, 16), step)
+        to = (gate_grad, up_grad, down_grad)[part]
+        return pltpu.make_async_copy(out.at[part, rows], to.at[rows], osem.at[3 * i + part])
+
+    sides = pltpu.make_async_copy(ab_h, ab, isem.at[n])
+    sides.start()
+    for i in range(n):
+        load(i).start()
+    sides.wait()
+
+    @pl.loop(0, n)
+    def _(i):
+        load(i).wait()
+        rows = pl.ds(pl.multiple_of(i * step, 16), step)
+        for part in range(3):
+            out[part, rows, :] = jnp.dot(
+                r[part, rows, :], ab[part // 2], preferred_element_type=F32
+            ).astype(BF16)
+            store(i, part).start()
+
+    for i in range(n):
+        for part in range(3):
+            store(i, part).wait()
 
 
 def grads(r, ab, width):
     depth = ab.shape[2]
-    step = 528
-    out = pl.BlockSpec((step, depth), lambda i: (i, 0))
+    assert width % GRAD_ROWS == 0
+    n = width // GRAD_ROWS
+    hbm = pl.BlockSpec(memory_space=pl.ANY)
     return pl.pallas_call(
         grads_kernel,
-        grid=(pl.cdiv(width, step),),
-        in_specs=[
-            pl.BlockSpec((3, step, 256), lambda i: (0, i, 0)),
-            pl.BlockSpec((2, 256, depth), lambda i: (0, 0, 0)),
+        in_specs=[hbm, hbm],
+        out_specs=(hbm, hbm, hbm),
+        out_shape=(pltpu.HBM((width, depth), BF16),) * 3,
+        scratch_shapes=[
+            pltpu.VMEM(r.shape, BF16),
+            pltpu.VMEM(ab.shape, BF16),
+            pltpu.VMEM((3, width, depth), BF16),
+            pltpu.SemaphoreType.DMA((n + 1,)),
+            pltpu.SemaphoreType.DMA((3 * n,)),
         ],
-        out_specs=(out, out, out),
-        out_shape=(jax.ShapeDtypeStruct((width, depth), BF16),) * 3,
-        compiler_params=pltpu.CompilerParams(vmem_limit_bytes=16 * 1024 * 1024),
+        compiler_params=pltpu.CompilerParams(vmem_limit_bytes=24 * 1024 * 1024),
         name="grads",
     )(r, ab)
 

time: 86.6 us -> 90.4 us (1.044)
  Pallas kernels: 85.2 us -> 88.4 us
    pallas_call x1, Pallas kernels: 78.5 us -> 81.1 us  [exchange(): pl.pallas_call(functools.partial(exchange_kernel, width), out_shape=(pltp...]
where the time goes in v6:
time: 90.4 us; the launch traced here: 89.7 us
  Pallas kernels  88.4 us (98%)
    pallas_call x1, Pallas kernels, exchange(): pl.pallas_call(functools.partial(exchange_kernel, width), out_shape=(pltp...  81.1 us
    pallas_call x1, Pallas kernels, grads(): pl.pallas_call(grads_kernel, in_specs=[hbm, hbm], out_specs=(hbm, hbm, hb...  7.26 us

profile of v6, /device:TPU:1, one launch (start us, length us, event | category | flops | bytes accessed | tf_op | source)
XLA Modules:
  0.0 89.7 jit_solution(3103627016581467898)
XLA Ops:
  0.6 81.1 %exchange.1 = (bf16[3,3712,256]{2,1,0:T(8,128)(2,1)S(1)}, bf16[2,256,512]{2,1,0:T(8,128)(2,1)S(1)}, f32[32,512]{1,0:T(8,128)}) custom-call(bf16[32,512]{1,0:T(8,128)(2,1)} %tok.1, bf16[32,512]{1,0:T(8,128)(2,1)} %og.1, f32[1,256]{1,0:T(1,128)} %bitcast.9, bf16[3696,512]{1,0:T(8,128)(2,1)} %bitcast.5, bf16[3696,512]{1,0:T(8,128)(2,1)} %bitcast.6, ...), custom_call_target="tpu_custom_call" | custom-call | flops 4844421120 | bytes 17031168 | tf_op jit(solution)/shard_map/exchange/pallas_call | solution.py:516
  81.8 0.0 copy-start
  81.8 7.3 %grads.1 = (bf16[3696,512]{1,0:T(8,128)(2,1)}, bf16[3696,512]{1,0:T(8,128)(2,1)}, bf16[3696,512]{1,0:T(8,128)(2,1)}) custom-call(bf16[3,3712,256]{2,1,0:T(8,128)(2,1)S(1)} %get-tuple-element.11.r_h, bf16[2,256,512]{2,1,0:T(8,128)(2,1)S(1)} %get-tuple-element.12.ab_h), custom_call_target="tpu_custom_call" | custom-call | tf_op jit(solution)/shard_map/grads/pallas_call | solution.py:601
  89.0 0.0 copy-done
  89.1 0.6 copy.11
Async XLA Ops:
  81.8 7.3 %copy-start = (f32[32,512]{1,0:T(8,128)S(1)}, f32[32,512]{1,0:T(8,128)}, u32[]{:S(2)}) copy-start(f32[32,512]{1,0:T(8,128)} %get-tuple-element.20) | copy-start | bytes 196612

commit v7 on v6

--- a/solution.py
+++ b/solution.py
@@ -209,22 +209,18 @@
 
         def block(half, lo, at, width):
             value = lax.dot_general(
-                ab[side, rows, :], wide[pl.ds(lo, width), :], NT, preferred_element_type=F32
+                ab[side, rows, :], wide[lo : lo + width, :], NT, preferred_element_type=F32
             )
             if kind == "T":
-                pf[:, :, :, :, pl.ds(at, width)] = value.reshape(2, 2, 4, 16, width)
+                pf[:, :, :, :, at : at + width] = value.reshape(2, 2, 4, 16, width)
             else:
-                pf[half, :, :, :, pl.ds(at, width)] = value.reshape(2, 4, 16, width)
+                pf[half, :, :, :, at : at + width] = value.reshape(2, 4, 16, width)
 
         for half in range(1 if kind == "T" else 2):
             lo = first + half * count
 
-            @pl.loop(0, count // 256)
-            def _(i):
-                block(half, pl.multiple_of(lo + i * 256, 128), pl.multiple_of(to + i * 256, 128), 256)
-
-            if count % 256:
-                block(half, lo + count - 128, to + count - 128, 128)
+            for at in range(0, count, 256):
+                block(half, lo + at, to + at, min(256, count - at))
 
     def products(j):
         kind, base_at, unit, size, _ = places[j]
@@ -444,22 +440,15 @@
     def transposes(j):
         kind, base_at, unit, size, _ = places[j]
         for part in range(3):
-            at = base_at + part * size
-
-            @pl.loop(0, size // LANE)
-            def _(i):
-                cols = pl.ds(pl.multiple_of(at + i * LANE, LANE), LANE)
-                if kind == "T":
-                    to = pl.ds(pl.multiple_of(unit + i * LANE, LANE), LANE)
-                    rt[part, to, :] = res[:, :, :, :, cols].reshape(256, LANE).T
-                else:
-                    start = 128 * (kind == "L")
-                    for half in range(2):
-                        to = pl.ds(pl.multiple_of(unit + half * size + i * LANE, LANE), LANE)
-                        rt[part, to, start : start + 128] = (
-                            res[half, :, :, :, cols].reshape(128, LANE).T
-                        )
-
+            cols = slice(base_at + part * size, base_at + part * size + size)
+            if kind == "T":
+                rt[part, unit : unit + size, :] = res[:, :, :, :, cols].reshape(256, size).T
+            else:
+                start = 128 * (kind == "L")
+                for lo, half in ((unit, 0), (unit + size, 1)):
+                    rt[part, lo : lo + size, start : start + 128] = (
+                        res[half, :, :, :, cols].reshape(128, size).T
+                    )
         if kind == "T":
             tokens, units = pl.ds(0, 256), pl.ds(unit, size)
         else:
@@ -578,10 +567,9 @@
         load(i).start()
     sides.wait()
 
-    @pl.loop(0, n)
-    def _(i):
+    for i in range(n):
         load(i).wait()
-        rows = pl.ds(pl.multiple_of(i * step, 16), step)
+        rows = slice(i * step, i * step + step)
         for part in range(3):
             out[part, rows, :] = jnp.dot(
                 r[part, rows, :], ab[part // 2], preferred_element_type=F32

time: 90.4 us -> 87.4 us (0.967)
  Pallas kernels: 88.4 us -> 86 us
    pallas_call x1, Pallas kernels: 81.1 us -> 78.5 us  [exchange(): pl.pallas_call(functools.partial(exchange_kernel, width), out_shape=(pltp...]
where the time goes in v7:
time: 87.4 us; the launch traced here: 87.3 us
  Pallas kernels  86 us (98%)
    pallas_call x1, Pallas kernels, exchange(): pl.pallas_call(functools.partial(exchange_kernel, width), out_shape=(pltp...  78.5 us
    pallas_call x1, Pallas kernels, grads(): pl.pallas_call(grads_kernel, in_specs=[hbm, hbm], out_specs=(hbm, hbm, hb...  7.44 us

profile of v7, /device:TPU:1, one launch (start us, length us, event | category | flops | bytes accessed | tf_op | source)
XLA Modules:
  0.0 87.3 jit_solution(4421590672562085949)
XLA Ops:
  0.6 78.5 %exchange.1 = (bf16[3,3712,256]{2,1,0:T(8,128)(2,1)S(1)}, bf16[2,256,512]{2,1,0:T(8,128)(2,1)S(1)}, f32[32,512]{1,0:T(8,128)}) custom-call(bf16[32,512]{1,0:T(8,128)(2,1)} %tok.1, bf16[32,512]{1,0:T(8,128)(2,1)} %og.1, f32[1,256]{1,0:T(1,128)} %bitcast.9, bf16[3696,512]{1,0:T(8,128)(2,1)} %bitcast.5, bf16[3696,512]{1,0:T(8,128)(2,1)} %bitcast.6, ...), custom_call_target="tpu_custom_call" | custom-call | flops 4844421120 | bytes 17031168 | tf_op jit(solution)/shard_map/exchange/pallas_call | solution.py:505
  79.2 0.0 copy-start
  79.2 7.4 %grads.1 = (bf16[3696,512]{1,0:T(8,128)(2,1)}, bf16[3696,512]{1,0:T(8,128)(2,1)}, bf16[3696,512]{1,0:T(8,128)(2,1)}) custom-call(bf16[3,3712,256]{2,1,0:T(8,128)(2,1)S(1)} %get-tuple-element.11.r_h, bf16[2,256,512]{2,1,0:T(8,128)(2,1)S(1)} %get-tuple-element.12.ab_h), custom_call_target="tpu_custom_call" | custom-call | tf_op jit(solution)/shard_map/grads/pallas_call | solution.py:589
  86.6 0.0 copy-done
  86.6 0.6 copy.11
Async XLA Ops:
  79.2 7.5 %copy-start = (f32[32,512]{1,0:T(8,128)S(1)}, f32[32,512]{1,0:T(8,128)}, u32[]{:S(2)}) copy-start(f32[32,512]{1,0:T(8,128)} %get-tuple-element.20) | copy-start | bytes 196612

commit v8 on v7

--- a/solution.py
+++ b/solution.py
@@ -11,26 +11,25 @@
 MESH = pl.DeviceIdType.MESH
 LANE = 128
 JOBS = (
-    ("E", 4, "zx", "zx"),
+    ("E", 4, "xz", "zx"),
     ("L", 4, "xz", "zx"),
-    ("T", 4, "zx", "xz"),
+    ("T", 5, "xz", "xz"),
+    ("T", 3, "xz", "xz"),
+    ("T", 3, "xz", "xz"),
+    ("T", 2, "zx", "xz"),
+    ("T", 5, "zx", "zx"),
     ("T", 3, "zx", "xz"),
-    ("T", 4, "xz", "zx"),
-    ("T", 3, "zx", "xz"),
-    ("T", 3, "zx", "xz"),
-    ("T", 2, "xz", "zx"),
-    ("T", 2, "zx", "zx"),
 )
 ORDER = (
-    (0, -1), (1, -1), (0, 0), (1, 0), (2, -1), (2, 0), (3, -1), (0, 1), (1, 1), (3, 0), (0, 2),
-    (1, 2), (0, 3), (1, 3), (2, 1), (0, 4), (2, 2), (4, 0), (1, 4), (0, 5), (2, 3), (1, 5), (0, 6),
-    (3, 2), (2, 4), (1, 6), (3, 1), (3, 3), (5, 0), (2, 5), (0, 7), (2, 6), (1, 7), (4, 2), (0, 8),
-    (4, 1), (1, 8), (4, 3), (2, 7), (3, 4), (6, 0), (2, 8), (3, 5), (5, 2), (3, 6), (5, 1), (5, 3),
-    (7, 0), (4, 4), (3, 8), (3, 7), (4, 5), (4, 6), (6, 2), (6, 1), (6, 3), (5, 4), (8, 0), (4, 7),
-    (4, 8), (5, 5), (5, 6), (7, 2), (9, 0), (7, 1), (10, 0), (7, 3), (6, 4), (5, 8), (6, 5), (5, 7),
-    (8, 2), (6, 6), (8, 1), (8, 3), (7, 4), (6, 8), (9, 2), (10, 2), (7, 5), (9, 1), (9, 3), (6, 7),
-    (10, 1), (8, 4), (7, 6), (7, 8), (10, 3), (8, 5), (7, 7), (9, 4), (8, 6), (8, 8), (10, 4),
-    (9, 5), (10, 5), (8, 7), (9, 6), (9, 8), (10, 6), (10, 8), (9, 7), (4, -1), (10, 7),
+    (0, -1), (1, -1), (0, 0), (1, 0), (2, -1), (2, 0), (3, -1), (0, 1), (1, 1), (0, 2), (1, 2),
+    (0, 3), (1, 3), (0, 4), (1, 4), (0, 5), (1, 5), (0, 6), (2, 1), (3, 0), (2, 2), (2, 3), (4, 0),
+    (2, 4), (2, 5), (1, 6), (0, 7), (3, 1), (5, 0), (3, 5), (1, 7), (4, 1), (2, 6), (6, 0), (3, 2),
+    (4, 5), (2, 7), (5, 1), (3, 6), (7, 0), (4, 2), (3, 3), (6, 1), (3, 4), (5, 5), (3, 7), (4, 6),
+    (5, 2), (7, 1), (8, 0), (4, 3), (6, 5), (4, 4), (5, 6), (9, 0), (6, 2), (5, 3), (7, 5), (4, 7),
+    (5, 4), (10, 0), (6, 6), (8, 1), (6, 3), (5, 7), (8, 5), (7, 2), (9, 1), (7, 6), (6, 4),
+    (10, 1), (9, 5), (7, 3), (6, 7), (10, 5), (8, 2), (7, 4), (8, 3), (9, 2), (10, 2), (7, 7),
+    (8, 6), (9, 3), (8, 4), (10, 3), (8, 7), (9, 6), (10, 6), (9, 4), (10, 4), (9, 7), (4, -1),
+    (10, 7),
 )
 NT = (((1,), (1,)), ((), ()))
 
@@ -46,7 +45,7 @@
         else:
             assert taken == pairs or taken == 0
             unit = max(pairs, units_end(out))
-        out.append((kind, at, unit, size, min(size, width - unit)))
+        out.append((kind, 0, unit, size, min(size, width - unit)))
         at += 3 * size
     assert taken == pairs and at == 3 * LANE * pl.cdiv(width, LANE)
     return out
@@ -57,20 +56,26 @@
 
 
 (
-    PAIR, PB, PC, PD, ZA, ZB, ZUP, ZDOWN, X1,
-    GUP, GDOWN, FUP, FDOWN, XA, XB, XC, XD, CA, CB, CC, CD,
-) = range(21)
-PER_CHUNK = 21
+    PAIR, PB, PC, PD, ZA, ZB, ZUP, ZDOWN, X1, GUP, GDOWN, FUP, FDOWN, XA, CA,
+) = range(15)
+PER_CHUNK = 15
 COLS = 9 + 8
+
+
+BUFFERS = (
+    ((2, 2, 4, 16), F32), ((2, 4, 16), F32),
+    ((2, 16), BF16), ((2, 16), BF16), ((2, 2, 16), BF16), ((2, 2, 16), BF16),
+    ((16,), F32), ((4, 16), BF16), ((4, 16), BF16), ((2, 2, 4, 16), BF16),
+)
 
 
 def exchange_kernel(
     width,
     tok, og, tw, wg_h, wu_h, wd_h,
     r_out, ab_out, ig_out,
-    wgu, wd, ab, pf, pr, zs1, zr1, zs2, zr2, own, xs, xr, res, rt, ig, igs, igr,
-    ssem, rsem, lsem, osem,
+    wgu, wd, ab, rt, ig, igs, igr, ssem, rsem, lsem, osem, *of_jobs,
 ):
+    pf, pr, zs1, zr1, zs2, zr2, own, xs, xr, res = (of_jobs[i :: 10] for i in range(10))
     places = places_of(width)
     n = len(places)
     row, k = lax.axis_index("row"), lax.axis_index("col")
@@ -212,9 +217,9 @@
                 ab[side, rows, :], wide[lo : lo + width, :], NT, preferred_element_type=F32
             )
             if kind == "T":
-                pf[:, :, :, :, at : at + width] = value.reshape(2, 2, 4, 16, width)
+                pf[j][:, :, :, :, at : at + width] = value.reshape(2, 2, 4, 16, width)
             else:
-                pf[half, :, :, :, at : at + width] = value.reshape(2, 4, 16, width)
+                pf[j][half, :, :, :, at : at + width] = value.reshape(2, 4, 16, width)
 
         for half in range(1 if kind == "T" else 2):
             lo = first + half * count
@@ -232,102 +237,108 @@
         _, base_at, unit, size, _ = places[j]
         m, cols = j * PER_CHUNK, span(j)
         multiply(j, 1, wd, unit, size, base_at + 2 * size)
-        if JOBS[j][2] == "zx":
+        if j > 0:
+            send(pf[j].at[1 - c], pr[j], m + PAIR, sib)
+        elif JOBS[j][2] == "zx":
             for zz, idx in ((zo, PAIR), (zp, PB), (zm, PC), (z, PD)):
-                send(pf.at[1 - c, :, zz, :, cols], pr.at[:, zz, :, cols], m + idx, sib)
+                send(pf[j].at[1 - c, :, zz, :, cols], pr[j].at[:, zz, :, cols], m + idx, sib)
         else:
             for xx, idx in ((1 - x, PAIR), (x, PB)):
-                send(pf.at[1 - c, xx, :, :, cols], pr.at[xx, :, :, cols], m + idx, sib)
-
-    def chip(xx, zz, cols):
-        return pf[c, xx, zz, :, cols] + pr[xx, zz, :, cols]
-
-    def chip_sum(xx, zz, cols):
-        return chip(xx, zz, cols) + xr[zz, :, cols].astype(F32)
+                send(pf[j].at[1 - c, xx, :, :, cols], pr[j].at[xx, :, :, cols], m + idx, sib)
+
+    def chip(j, xx, zz, cols):
+        return pf[j][c, xx, zz, :, cols] + pr[j][xx, zz, :, cols]
+
+    def chip_sum(j, xx, zz, cols):
+        return chip(j, xx, zz, cols) + xr[j][zz, :, cols].astype(F32)
 
     def zx_far(j):
         m, cols = j * PER_CHUNK, span(j)
-        landed(pr.at[:, zo, :, cols], m + PAIR)
-        zs1[0, :, cols] = chip(0, zo, cols).astype(BF16)
-        send(zs1.at[0, :, cols], zr1.at[0, :, cols], m + ZA, up)
-        zs1[1, :, cols] = chip(1, zo, cols).astype(BF16)
-        send(zs1.at[1, :, cols], zr1.at[1, :, cols], m + ZB, down)
+        landed(pr[j] if j > 0 else pr[j].at[:, zo], m + PAIR)
+        zs1[j][0, :, cols] = chip(j, 0, zo, cols).astype(BF16)
+        send(zs1[j].at[0, :, cols], zr1[j].at[0, :, cols], m + ZA, up)
+        zs1[j][1, :, cols] = chip(j, 1, zo, cols).astype(BF16)
+        send(zs1[j].at[1, :, cols], zr1[j].at[1, :, cols], m + ZB, down)
 
     def zx_near(j):
         m, cols = j * PER_CHUNK, span(j)
-        landed(pr.at[:, zp, :, cols], m + PB)
-        landed(zr1.at[0, :, cols], m + ZA)
-        zs2[0, 0, :, cols] = (chip(0, zp, cols) + zr1[0, :, cols].astype(F32)).astype(BF16)
-        zs2[0, 1, :, cols] = chip(1, zp, cols).astype(BF16)
-        send(zs2.at[0, :, :, cols], zr2.at[0, :, :, cols], m + ZUP, up)
-        landed(pr.at[:, zm, :, cols], m + PC)
-        landed(zr1.at[1, :, cols], m + ZB)
-        zs2[1, 0, :, cols] = chip(0, zm, cols).astype(BF16)
-        zs2[1, 1, :, cols] = (chip(1, zm, cols) + zr1[1, :, cols].astype(F32)).astype(BF16)
-        send(zs2.at[1, :, :, cols], zr2.at[1, :, :, cols], m + ZDOWN, down)
+        if j == 0:
+            landed(pr[j].at[:, zp], m + PB)
+        landed(zr1[j].at[0, :, cols], m + ZA)
+        zs2[j][0, 0, :, cols] = (chip(j, 0, zp, cols) + zr1[j][0, :, cols].astype(F32)).astype(BF16)
+        zs2[j][0, 1, :, cols] = chip(j, 1, zp, cols).astype(BF16)
+        send(zs2[j].at[0, :, :, cols], zr2[j].at[0, :, :, cols], m + ZUP, up)
+        if j == 0:
+            landed(pr[j].at[:, zm], m + PC)
+        landed(zr1[j].at[1, :, cols], m + ZB)
+        zs2[j][1, 0, :, cols] = chip(j, 0, zm, cols).astype(BF16)
+        zs2[j][1, 1, :, cols] = (chip(j, 1, zm, cols) + zr1[j][1, :, cols].astype(F32)).astype(BF16)
+        send(zs2[j].at[1, :, :, cols], zr2[j].at[1, :, :, cols], m + ZDOWN, down)
 
     def zx_cross(j):
         m, cols = j * PER_CHUNK, span(j)
-        landed(pr.at[:, z, :, cols], m + PD)
-        landed(zr2.at[0, :, :, cols], m + ZUP)
-        landed(zr2.at[1, :, :, cols], m + ZDOWN)
+        if j == 0:
+            landed(pr[j].at[:, z], m + PD)
+        landed(zr2[j].at[0, :, :, cols], m + ZUP)
+        landed(zr2[j].at[1, :, :, cols], m + ZDOWN)
 
         def ring(xx):
-            return chip(xx, z, cols) + zr2[0, xx, :, cols].astype(F32) + zr2[1, xx, :, cols].astype(F32)
-
-        xs[0, :, cols] = ring(1 - x).astype(BF16)
-        send(xs.at[0, :, cols], xr.at[0, :, cols], m + X1, xn)
-        own[:, cols] = ring(x)
+            return chip(j, xx, z, cols) + zr2[j][0, xx, :, cols].astype(F32) + zr2[j][1, xx, :, cols].astype(F32)
+
+        xs[j][0, :, cols] = ring(1 - x).astype(BF16)
+        send(xs[j].at[0, :, cols], xr[j].at[0, :, cols], m + X1, xn)
+        own[j][:, cols] = ring(x)
 
     def zx_total(j):
         m, cols = j * PER_CHUNK, span(j)
-        landed(xr.at[0, :, cols], m + X1)
-        return lambda at: own[:, at] + xr[0, :, at].astype(F32)
+        landed(xr[j].at[0, :, cols], m + X1)
+        return lambda at: own[j][:, at] + xr[j][0, :, at].astype(F32)
 
     def xz_cross(j):
         m, cols = j * PER_CHUNK, span(j)
-        landed(pr.at[1 - x, :, :, cols], m + PAIR)
-        xs[:, :, cols] = (pf[c, 1 - x, :, :, cols] + pr[1 - x, :, :, cols]).astype(BF16)
-        send(xs.at[:, :, cols], xr.at[:, :, cols], m + X1, xn)
+        landed(pr[j] if j > 0 else pr[j].at[1 - x], m + PAIR)
+        xs[j][:, :, cols] = (pf[j][c, 1 - x, :, :, cols] + pr[j][1 - x, :, :, cols]).astype(BF16)
+        send(xs[j].at[:, :, cols], xr[j].at[:, :, cols], m + X1, xn)
 
     def xz_far(j):
         m, cols = j * PER_CHUNK, span(j)
         lo, hi = halves(j)
-        landed(pr.at[x, :, :, cols], m + PB)
-        landed(xr.at[:, :, cols], m + X1)
-        zs1[0, :, lo] = chip_sum(x, zo, lo).astype(BF16)
-        send(zs1.at[0, :, lo], zr1.at[0, :, lo], m + ZA, up)
-        zs1[1, :, hi] = chip_sum(x, zo, hi).astype(BF16)
-        send(zs1.at[1, :, hi], zr1.at[1, :, hi], m + ZB, down)
+        if j == 0:
+            landed(pr[j].at[x], m + PB)
+        landed(xr[j].at[:, :, cols], m + X1)
+        zs1[j][0, :, lo] = chip_sum(j, x, zo, lo).astype(BF16)
+        send(zs1[j].at[0, :, lo], zr1[j].at[0, :, lo], m + ZA, up)
+        zs1[j][1, :, hi] = chip_sum(j, x, zo, hi).astype(BF16)
+        send(zs1[j].at[1, :, hi], zr1[j].at[1, :, hi], m + ZB, down)
 
     def xz_near(j):
         m, cols = j * PER_CHUNK, span(j)
         lo, hi = halves(j)
-        landed(zr1.at[0, :, lo], m + ZA)
-        zs2[0, 0, :, lo] = (chip_sum(x, zp, lo) + zr1[0, :, lo].astype(F32)).astype(BF16)
-        zs2[0, 0, :, hi] = chip_sum(x, zp, hi).astype(BF16)
-        send(zs2.at[0, 0, :, cols], zr2.at[0, 0, :, cols], m + ZUP, up)
-        landed(zr1.at[1, :, hi], m + ZB)
-        zs2[1, 0, :, lo] = chip_sum(x, zm, lo).astype(BF16)
-        zs2[1, 0, :, hi] = (chip_sum(x, zm, hi) + zr1[1, :, hi].astype(F32)).astype(BF16)
-        send(zs2.at[1, 0, :, cols], zr2.at[1, 0, :, cols], m + ZDOWN, down)
+        landed(zr1[j].at[0, :, lo], m + ZA)
+        zs2[j][0, 0, :, lo] = (chip_sum(j, x, zp, lo) + zr1[j][0, :, lo].astype(F32)).astype(BF16)
+        zs2[j][0, 0, :, hi] = chip_sum(j, x, zp, hi).astype(BF16)
+        send(zs2[j].at[0, 0, :, cols], zr2[j].at[0, 0, :, cols], m + ZUP, up)
+        landed(zr1[j].at[1, :, hi], m + ZB)
+        zs2[j][1, 0, :, lo] = chip_sum(j, x, zm, lo).astype(BF16)
+        zs2[j][1, 0, :, hi] = (chip_sum(j, x, zm, hi) + zr1[j][1, :, hi].astype(F32)).astype(BF16)
+        send(zs2[j].at[1, 0, :, cols], zr2[j].at[1, 0, :, cols], m + ZDOWN, down)
 
     def xz_total(j):
         m, cols = j * PER_CHUNK, span(j)
-        landed(zr2.at[0, 0, :, cols], m + ZUP)
-        landed(zr2.at[1, 0, :, cols], m + ZDOWN)
+        landed(zr2[j].at[0, 0, :, cols], m + ZUP)
+        landed(zr2[j].at[1, 0, :, cols], m + ZDOWN)
         return lambda at: (
-            chip_sum(x, z, at) + zr2[0, 0, :, at].astype(F32) + zr2[1, 0, :, at].astype(F32)
+            chip_sum(j, x, z, at) + zr2[j][0, 0, :, at].astype(F32) + zr2[j][1, 0, :, at].astype(F32)
         )
 
-    def here(xx, zz, cols):
-        return res.at[c, xx, zz, :, cols]
-
-    def push(xx, zz, cols, idx, dev):
-        send(here(xx, zz, cols), here(xx, zz, cols), idx, dev)
-
-    def push_pair(zz, cols, idx, dev):
-        part = res.at[c, :, zz, :, cols]
+    def here(j, xx, zz, cols):
+        return res[j].at[c, xx, zz, :, cols]
+
+    def push(j, xx, zz, cols, idx, dev):
+        send(here(j, xx, zz, cols), here(j, xx, zz, cols), idx, dev)
+
+    def push_pair(j, zz, cols, idx, dev):
+        part = res[j].at[c, :, zz, :, cols]
         send(part, part, idx, dev)
 
     def activate(j):
@@ -348,78 +359,60 @@
             scaled * silu,
             column * (silu * linear),
         )):
-            res[c, x, z, :, place(part)] = value.astype(BF16)
-        push(x, z, cols, m + XA, xn)
+            res[j][c, x, z, :, place(part)] = value.astype(BF16)
         if JOBS[j][3] == "zx":
-            push(x, z, cols, m + GUP, up)
-            push(x, z, cols, m + GDOWN, down)
+            push(j, x, z, cols, m + GUP, up)
+            push(j, x, z, cols, m + GDOWN, down)
+        else:
+            push(j, x, z, cols, m + XA, xn)
 
     def zx_gather_near(j):
         m, cols = j * PER_CHUNK, span(j)
         lo, hi = halves(j)
-        landed(here(x, zm, cols), m + GUP)
-        push(x, zm, lo, m + FUP, up)
-        push(x, zm, cols, m + XB, xn)
-        landed(here(x, zp, cols), m + GDOWN)
-        push(x, zp, hi, m + FDOWN, down)
-        push(x, zp, cols, m + XC, xn)
+        landed(here(j, x, zm, cols), m + GUP)
+        push(j, x, zm, lo, m + FUP, up)
+        landed(here(j, x, zp, cols), m + GDOWN)
+        push(j, x, zp, hi, m + FDOWN, down)
 
     def zx_gather_far(j):
-        m, cols = j * PER_CHUNK, span(j)
+        m = j * PER_CHUNK
         lo, hi = halves(j)
-        landed(here(x, zo, lo), m + FUP)
-        landed(here(x, zo, hi), m + FDOWN)
-        push(x, zo, cols, m + XD, xn)
-        part = res.at[c, x, :, :, cols]
+        landed(here(j, x, zo, lo), m + FUP)
+        landed(here(j, x, zo, hi), m + FDOWN)
+        part = res[j].at[c, x]
+        send(part, part, m + XA, xn)
+
+    def zx_gather_cross(j):
+        landed(res[j].at[c, 1 - x], j * PER_CHUNK + XA)
+        part = res[j].at[c]
+        send(part, part, j * PER_CHUNK + CA, sib)
+
+    def xz_gather_cross(j):
+        m, cols = j * PER_CHUNK, span(j)
+        landed(here(j, 1 - x, z, cols), m + XA)
+        push_pair(j, z, cols, m + GUP, up)
+        push_pair(j, z, cols, m + GDOWN, down)
+
+    def xz_gather_near(j):
+        m, cols = j * PER_CHUNK, span(j)
+        landed(res[j].at[c, :, zm, :, cols], m + GUP)
+        push(j, 0, zm, cols, m + FUP, up)
+        landed(res[j].at[c, :, zp, :, cols], m + GDOWN)
+        push(j, 1, zp, cols, m + FDOWN, down)
+
+    def xz_gather_far(j):
+        m, cols = j * PER_CHUNK, span(j)
+        landed(here(j, 0, zo, cols), m + FUP)
+        landed(here(j, 1, zo, cols), m + FDOWN)
+        part = res[j].at[c]
         send(part, part, m + CA, sib)
-
-    def zx_gather_cross(j):
-        m, cols = j * PER_CHUNK, span(j)
-        landed(here(1 - x, z, cols), m + XA)
-        landed(here(1 - x, zm, cols), m + XB)
-        landed(here(1 - x, zp, cols), m + XC)
-        landed(here(1 - x, zo, cols), m + XD)
-        part = res.at[c, 1 - x, :, :, cols]
-        send(part, part, m + CB, sib)
-
-    def zx_all(j):
-        m, cols = j * PER_CHUNK, span(j)
-        landed(res.at[1 - c, x, :, :, cols], m + CA)
-        landed(res.at[1 - c, 1 - x, :, :, cols], m + CB)
-
-    def xz_gather_cross(j):
-        m, cols = j * PER_CHUNK, span(j)
-        landed(here(1 - x, z, cols), m + XA)
-        push_pair(z, cols, m + GUP, up)
-        push_pair(z, cols, m + GDOWN, down)
-        push_pair(z, cols, m + CA, sib)
-
-    def xz_gather_near(j):
-        m, cols = j * PER_CHUNK, span(j)
-        landed(res.at[c, :, zm, :, cols], m + GUP)
-        push(0, zm, cols, m + FUP, up)
-        landed(res.at[c, :, zp, :, cols], m + GDOWN)
-        push(1, zp, cols, m + FDOWN, down)
-        push_pair(zm, cols, m + CB, sib)
-        push_pair(zp, cols, m + CC, sib)
-
-    def xz_gather_far(j):
-        m, cols = j * PER_CHUNK, span(j)
-        landed(here(0, zo, cols), m + FUP)
-        landed(here(1, zo, cols), m + FDOWN)
-        push_pair(zo, cols, m + CD, sib)
-
-    def xz_all(j):
-        m, cols = j * PER_CHUNK, span(j)
-        for zz, idx in ((z, CA), (zm, CB), (zp, CC), (zo, CD)):
-            landed(res.at[1 - c, :, zz, :, cols], m + idx)
 
     def finish(j):
         kind, base_at, unit, size, _ = places[j]
-        (zx_all if JOBS[j][3] == "zx" else xz_all)(j)
+        landed(res[j].at[1 - c], j * PER_CHUNK + CA)
         at = slice(base_at, base_at + 2 * size)
         if kind == "T":
-            piece = res[:, :, :, :, at].reshape(256, 2 * size)
+            piece = res[j][:, :, :, :, at].reshape(256, 2 * size)
             ig[...] += jnp.dot(
                 piece, wgu[2 * unit : 2 * unit + 2 * size, :], preferred_element_type=F32
             )
@@ -427,12 +420,12 @@
             start = 128 * (kind == "L")
             lo = 2 * unit
             value = jnp.dot(
-                res[0, :, :, :, at].reshape(128, 2 * size), wgu[lo : lo + 2 * size, :],
+                res[j][0, :, :, :, at].reshape(128, 2 * size), wgu[lo : lo + 2 * size, :],
                 preferred_element_type=F32,
             )
             lo += 2 * size
             value += jnp.dot(
-                res[1, :, :, :, at].reshape(128, 2 * size), wgu[lo : lo + 2 * size, :],
+                res[j][1, :, :, :, at].reshape(128, 2 * size), wgu[lo : lo + 2 * size, :],
                 preferred_element_type=F32,
             )
             ig[start : start + 128, :] += value
@@ -442,12 +435,12 @@
         for part in range(3):
             cols = slice(base_at + part * size, base_at + part * size + size)
             if kind == "T":
-                rt[part, unit : unit + size, :] = res[:, :, :, :, cols].reshape(256, size).T
+                rt[part, unit : unit + size, :] = res[j][:, :, :, :, cols].reshape(256, size).T
             else:
                 start = 128 * (kind == "L")
                 for lo, half in ((unit, 0), (unit + size, 1)):
                     rt[part, lo : lo + size, start : start + 128] = (
-                        res[half, :, :, :, cols].reshape(128, size).T
+                        res[j][half, :, :, :, cols].reshape(128, size).T
                     )
         if kind == "T":
             tokens, units = pl.ds(0, 256), pl.ds(unit, size)
@@ -497,7 +490,6 @@
 def exchange(tokens, out_grad, token_weight, gate_weight, up_weight, down_weight):
     width, depth = gate_weight.shape
     wide = pl.cdiv(width, LANE) * LANE
-    cols = 3 * wide
     n = len(JOBS)
     messages = n * PER_CHUNK + COLS
     hbm = pl.BlockSpec(memory_space=pl.ANY)
@@ -515,16 +507,6 @@
             pltpu.VMEM((2 * wide, depth), BF16),
             pltpu.VMEM((wide, depth), BF16),
             pltpu.VMEM((2, 256, depth), BF16),
-            pltpu.VMEM((2, 2, 4, 16, cols), F32),
-            pltpu.VMEM((2, 4, 16, cols), F32),
-            pltpu.VMEM((2, 16, cols), BF16),
-            pltpu.VMEM((2, 16, cols), BF16),
-            pltpu.VMEM((2, 2, 16, cols), BF16),
-            pltpu.VMEM((2, 2, 16, cols), BF16),
-            pltpu.VMEM((16, cols), F32),
-            pltpu.VMEM((4, 16, cols), BF16),
-            pltpu.VMEM((4, 16, cols), BF16),
-            pltpu.VMEM((2, 2, 4, 16, cols), BF16),
             pltpu.VMEM((3, wide, 256), BF16),
             pltpu.VMEM((256, depth), F32),
             pltpu.VMEM((256, depth), BF16),
@@ -533,6 +515,11 @@
             pltpu.SemaphoreType.DMA((messages,)),
             pltpu.SemaphoreType.DMA((2 + 6 * n,)),
             pltpu.SemaphoreType.DMA((1 + n,)),
+            *(
+                pltpu.VMEM((*dims, 3 * tiles * LANE), dtype)
+                for _, tiles, _, _ in JOBS
+                for dims, dtype in BUFFERS
+            ),
         ],
         compiler_params=pltpu.CompilerParams(
             collective_id=0, has_side_effects=True, vmem_limit_bytes=50 * 1024 * 1024
@@ -548,28 +535,18 @@
 GRAD_ROWS = 336
 
 
-def grads_kernel(r_h, ab_h, gate_grad, up_grad, down_grad, r, ab, out, isem, osem):
+def grads_kernel(r, ab, gate_grad, up_grad, down_grad, out, osem):
     step = GRAD_ROWS
     n = gate_grad.shape[0] // step
-
-    def load(i):
-        rows = pl.ds(pl.multiple_of(i * step, 16), step)
-        return pltpu.make_async_copy(r_h.at[:, rows], r.at[:, rows], isem.at[i])
 
     def store(i, part):
         rows = pl.ds(pl.multiple_of(i * step, 16), step)
         to = (gate_grad, up_grad, down_grad)[part]
         return pltpu.make_async_copy(out.at[part, rows], to.at[rows], osem.at[3 * i + part])
 
-    sides = pltpu.make_async_copy(ab_h, ab, isem.at[n])
-    sides.start()
-    for i in range(n):
-        load(i).start()
-    sides.wait()
-
-    for i in range(n):
-        load(i).wait()
-        rows = slice(i * step, i * step + step)
+    @pl.loop(0, n)
+    def _(i):
+        rows = pl.ds(pl.multiple_of(i * step, 16), step)
         for part in range(3):
             out[part, rows, :] = jnp.dot(
                 r[part, rows, :], ab[part // 2], preferred_element_type=F32
@@ -586,16 +563,14 @@
     assert width % GRAD_ROWS == 0
     n = width // GRAD_ROWS
     hbm = pl.BlockSpec(memory_space=pl.ANY)
+    vmem = pl.BlockSpec(memory_space=pltpu.VMEM)
     return pl.pallas_call(
         grads_kernel,
-        in_specs=[hbm, hbm],
+        in_specs=[vmem, vmem],
         out_specs=(hbm, hbm, hbm),
         out_shape=(pltpu.HBM((width, depth), BF16),) * 3,
         scratch_shapes=[
-            pltpu.VMEM(r.shape, BF16),
-            pltpu.VMEM(ab.shape, BF16),
             pltpu.VMEM((3, width, depth), BF16),
-            pltpu.SemaphoreType.DMA((n + 1,)),
             pltpu.SemaphoreType.DMA((3 * n,)),
         ],
         compiler_params=pltpu.CompilerParams(vmem_limit_bytes=24 * 1024 * 1024),

time: 87.4 us -> 87.8 us (level)
    pallas_call x1, Pallas kernels: 78.5 us -> 80.5 us  [exchange(): pl.pallas_call(functools.partial(exchange_kernel, width), out_shape=(pltp...]
    pallas_call x1, Pallas kernels: 7.44 us -> 5.84 us  [grads(): pl.pallas_call(grads_kernel, in_specs=[vmem, vmem], out_specs=(hbm, hbm,...]
where the time goes in v8:
time: 87.8 us; the launch traced here: 87.6 us
  Pallas kernels  86.3 us (98%)
    pallas_call x1, Pallas kernels, exchange(): pl.pallas_call(functools.partial(exchange_kernel, width), out_shape=(pltp...  80.5 us
    pallas_call x1, Pallas kernels, grads(): pl.pallas_call(grads_kernel, in_specs=[vmem, vmem], out_specs=(hbm, hbm,...  5.84 us

profile of v8, /device:TPU:1, one launch (start us, length us, event | category | flops | bytes accessed | tf_op | source)
XLA Modules:
  0.0 87.6 jit_solution(16672221887341367216)
XLA Ops:
  0.6 80.5 %exchange.1 = (bf16[3,3712,256]{2,1,0:T(8,128)(2,1)S(1)}, bf16[2,256,512]{2,1,0:T(8,128)(2,1)S(1)}, f32[32,512]{1,0:T(8,128)}) custom-call(bf16[32,512]{1,0:T(8,128)(2,1)} %tok.1, bf16[32,512]{1,0:T(8,128)(2,1)} %og.1, f32[1,256]{1,0:T(1,128)} %bitcast.9, bf16[3696,512]{1,0:T(8,128)(2,1)} %bitcast.5, bf16[3696,512]{1,0:T(8,128)(2,1)} %bitcast.6, ...), custom_call_target="tpu_custom_call" | custom-call | flops 4844421120 | bytes 17031168 | tf_op jit(solution)/shard_map/exchange/pallas_call | solution.py:497
  81.1 0.0 copy-start
  81.1 5.8 %grads.1 = (bf16[3696,512]{1,0:T(8,128)(2,1)}, bf16[3696,512]{1,0:T(8,128)(2,1)}, bf16[3696,512]{1,0:T(8,128)(2,1)}) custom-call(bf16[3,3712,256]{2,1,0:T(8,128)(2,1)S(1)} %get-tuple-element.11.r, bf16[2,256,512]{2,1,0:T(8,128)(2,1)S(1)} %get-tuple-element.12.ab), custom_call_target="tpu_custom_call" | custom-call | tf_op jit(solution)/shard_map/grads/pallas_call | solution.py:567
  87.0 0.0 copy-done
  87.0 0.6 copy.11
Async XLA Ops:
  81.1 5.9 %copy-start = (f32[32,512]{1,0:T(8,128)S(1)}, f32[32,512]{1,0:T(8,128)}, u32[]{:S(2)}) copy-start(f32[32,512]{1,0:T(8,128)} %get-tuple-element.20) | copy-start | bytes 196612

commit v9 on v7

--- a/solution.py
+++ b/solution.py
@@ -123,18 +123,17 @@
                     src.at[pl.ds(lo, valid)], dst.at[pl.ds(to, valid)],
                     lsem.at[2 + 6 * j + len(weights[j])],
                 ))
-                if valid < size:
-                    dst[to + valid : to + size, :] = jnp.zeros((size - valid, dst.shape[1]), BF16)
-    for copy in first + sum(weights, []):
+
+    for copy in first:
         copy.start()
-
     barrier = pltpu.get_barrier_semaphore()
     greeted = [sib, xn, up, down]
     for slot in range(1, 8):
         greeted.append(cdev(*owner(slot)))
     for dev in greeted:
         pl.semaphore_signal(barrier, inc=1, device_id=dev, device_id_type=MESH)
-    ig[...] = jnp.zeros_like(ig)
+    for copy in weights[0]:
+        copy.start()
     for copy in first:
         copy.wait()
     pl.semaphore_wait(barrier, len(greeted))
@@ -150,6 +149,16 @@
     send(both(0), both(3), base + 2, cdev(y, 1 - h))
     send(both(0), both(1), base + 0, cdev(yp, h))
     send(both(0), both(2), base + 1, cdev(ym, h))
+    for copy in sum(weights[1:], []):
+        copy.start()
+    kind, _, unit, size, valid = places[-1]
+    assert kind == "T" and all(place[3] == place[4] for place in places[:-1])
+    if valid < size:
+        rows = jnp.zeros((size - valid, wd.shape[1]), BF16)
+        wgu[2 * unit + valid : 2 * unit + size, :] = rows
+        wgu[2 * unit + size + valid : 2 * unit + 2 * size, :] = rows
+        wd[unit + valid : unit + size, :] = rows
+    ig[...] = jnp.zeros_like(ig)
 
     def col_near():
         landed(both(1), base + 0)
@@ -461,7 +470,7 @@
 
     def col_send():
         igs[...] = ig[...].astype(BF16)
-        for slot in range(1, 8):
+        for slot in (3, 7, 4, 5, 6, 1, 2):
             send(
                 igs.at[slot * 32 : slot * 32 + 32], igr.at[slot], base + 9 + slot,
                 cdev(*owner(slot)),
@@ -482,16 +491,18 @@
                 products, back_products, *reduce[over], activate, *gather[back], finish, transposes,
             )[stage](j)
 
+    for copy in sent[:-7]:
+        copy.wait_send()
+    for copy in outs:
+        copy.wait()
     total = ig[:32, :]
     for slot in range(1, 8):
         landed(igr.at[slot], base + 9 + slot)
         total = total + igr[slot].astype(F32)
     ig_out[...] = total
 
-    for copy in sent:
+    for copy in sent[-7:]:
         copy.wait_send()
-    for copy in outs:
-        copy.wait()
 
 
 def exchange(tokens, out_grad, token_weight, gate_weight, up_weight, down_weight):
@@ -548,28 +559,18 @@
 GRAD_ROWS = 336
 
 
-def grads_kernel(r_h, ab_h, gate_grad, up_grad, down_grad, r, ab, out, isem, osem):
+def grads_kernel(r, ab, gate_grad, up_grad, down_grad, out, osem):
     step = GRAD_ROWS
     n = gate_grad.shape[0] // step
-
-    def load(i):
-        rows = pl.ds(pl.multiple_of(i * step, 16), step)
-        return pltpu.make_async_copy(r_h.at[:, rows], r.at[:, rows], isem.at[i])
 
     def store(i, part):
         rows = pl.ds(pl.multiple_of(i * step, 16), step)
         to = (gate_grad, up_grad, down_grad)[part]
         return pltpu.make_async_copy(out.at[part, rows], to.at[rows], osem.at[3 * i + part])
 
-    sides = pltpu.make_async_copy(ab_h, ab, isem.at[n])
-    sides.start()
-    for i in range(n):
-        load(i).start()
-    sides.wait()
-
-    for i in range(n):
-        load(i).wait()
-        rows = slice(i * step, i * step + step)
+    @pl.loop(0, n)
+    def _(i):
+        rows = pl.ds(pl.multiple_of(i * step, 16), step)
         for part in range(3):
             out[part, rows, :] = jnp.dot(
                 r[part, rows, :], ab[part // 2], preferred_element_type=F32
@@ -586,16 +587,14 @@
     assert width % GRAD_ROWS == 0
     n = width // GRAD_ROWS
     hbm = pl.BlockSpec(memory_space=pl.ANY)
+    vmem = pl.BlockSpec(memory_space=pltpu.VMEM)
     return pl.pallas_call(
         grads_kernel,
-        in_specs=[hbm, hbm],
+        in_specs=[vmem, vmem],
         out_specs=(hbm, hbm, hbm),
         out_shape=(pltpu.HBM((width, depth), BF16),) * 3,
         scratch_shapes=[
-            pltpu.VMEM(r.shape, BF16),
-            pltpu.VMEM(ab.shape, BF16),
             pltpu.VMEM((3, width, depth), BF16),
-            pltpu.SemaphoreType.DMA((n + 1,)),
             pltpu.SemaphoreType.DMA((3 * n,)),
         ],
         compiler_params=pltpu.CompilerParams(vmem_limit_bytes=24 * 1024 * 1024),

time: 87.4 us -> 85.2 us (0.975)
  Pallas kernels: 86 us -> 83.8 us
    pallas_call x1, Pallas kernels: 7.44 us -> 5.84 us  [grads(): pl.pallas_call(grads_kernel, in_specs=[vmem, vmem], out_specs=(hbm, hbm,...]
where the time goes in v9:
time: 85.2 us; the launch traced here: 85.1 us
  Pallas kernels  83.8 us (98%)
    pallas_call x1, Pallas kernels, exchange(): pl.pallas_call(functools.partial(exchange_kernel, width), out_shape=(pltp...  78 us
    pallas_call x1, Pallas kernels, grads(): pl.pallas_call(grads_kernel, in_specs=[vmem, vmem], out_specs=(hbm, hbm,...  5.84 us

profile of v9, /device:TPU:1, one launch (start us, length us, event | category | flops | bytes accessed | tf_op | source)
XLA Modules:
  0.0 85.1 jit_solution(10968986340599544217)
XLA Ops:
  0.6 78.0 %exchange.1 = (bf16[3,3712,256]{2,1,0:T(8,128)(2,1)S(1)}, bf16[2,256,512]{2,1,0:T(8,128)(2,1)S(1)}, f32[32,512]{1,0:T(8,128)}) custom-call(bf16[32,512]{1,0:T(8,128)(2,1)} %tok.1, bf16[32,512]{1,0:T(8,128)(2,1)} %og.1, f32[1,256]{1,0:T(1,128)} %bitcast.9, bf16[3696,512]{1,0:T(8,128)(2,1)} %bitcast.5, bf16[3696,512]{1,0:T(8,128)(2,1)} %bitcast.6, ...), custom_call_target="tpu_custom_call" | custom-call | flops 4844421120 | bytes 17031168 | tf_op jit(solution)/shard_map/exchange/pallas_call | solution.py:516
  78.6 0.0 copy-start
  78.6 5.8 %grads.1 = (bf16[3696,512]{1,0:T(8,128)(2,1)}, bf16[3696,512]{1,0:T(8,128)(2,1)}, bf16[3696,512]{1,0:T(8,128)(2,1)}) custom-call(bf16[3,3712,256]{2,1,0:T(8,128)(2,1)S(1)} %get-tuple-element.11.r, bf16[2,256,512]{2,1,0:T(8,128)(2,1)S(1)} %get-tuple-element.12.ab), custom_call_target="tpu_custom_call" | custom-call | tf_op jit(solution)/shard_map/grads/pallas_call | solution.py:591
  84.5 0.0 copy-done
  84.5 0.6 copy.11
Async XLA Ops:
  78.6 5.9 %copy-start = (f32[32,512]{1,0:T(8,128)S(1)}, f32[32,512]{1,0:T(8,128)}, u32[]{:S(2)}) copy-start(f32[32,512]{1,0:T(8,128)} %get-tuple-element.20) | copy-start | bytes 196612

commit v10 on v9

--- a/solution.py
+++ b/solution.py
@@ -11,26 +11,24 @@
 MESH = pl.DeviceIdType.MESH
 LANE = 128
 JOBS = (
-    ("E", 4, "zx", "zx"),
-    ("L", 4, "xz", "zx"),
-    ("T", 4, "zx", "xz"),
-    ("T", 3, "zx", "xz"),
-    ("T", 4, "xz", "zx"),
-    ("T", 3, "zx", "xz"),
-    ("T", 3, "zx", "xz"),
-    ("T", 2, "xz", "zx"),
-    ("T", 2, "zx", "zx"),
+    ("E", 4, "xz", "zx"),
+    ("L", 4, "xz", "xz"),
+    ("T", 5, "zx", "zx"),
+    ("T", 3, "xz", "xz"),
+    ("T", 5, "xz", "xz"),
+    ("T", 5, "zx", "zx"),
+    ("T", 1, "zx", "zx"),
+    ("T", 2, "zx", "xz"),
 )
 ORDER = (
-    (0, -1), (1, -1), (0, 0), (1, 0), (2, -1), (2, 0), (3, -1), (0, 1), (1, 1), (3, 0), (0, 2),
-    (1, 2), (0, 3), (1, 3), (2, 1), (0, 4), (2, 2), (4, 0), (1, 4), (0, 5), (2, 3), (1, 5), (0, 6),
-    (3, 2), (2, 4), (1, 6), (3, 1), (3, 3), (5, 0), (2, 5), (0, 7), (2, 6), (1, 7), (4, 2), (0, 8),
-    (4, 1), (1, 8), (4, 3), (2, 7), (3, 4), (6, 0), (2, 8), (3, 5), (5, 2), (3, 6), (5, 1), (5, 3),
-    (7, 0), (4, 4), (3, 8), (3, 7), (4, 5), (4, 6), (6, 2), (6, 1), (6, 3), (5, 4), (8, 0), (4, 7),
-    (4, 8), (5, 5), (5, 6), (7, 2), (9, 0), (7, 1), (10, 0), (7, 3), (6, 4), (5, 8), (6, 5), (5, 7),
-    (8, 2), (6, 6), (8, 1), (8, 3), (7, 4), (6, 8), (9, 2), (10, 2), (7, 5), (9, 1), (9, 3), (6, 7),
-    (10, 1), (8, 4), (7, 6), (7, 8), (10, 3), (8, 5), (7, 7), (9, 4), (8, 6), (8, 8), (10, 4),
-    (9, 5), (10, 5), (8, 7), (9, 6), (9, 8), (10, 6), (10, 8), (9, 7), (4, -1), (10, 7),
+    (0, -1), (1, -1), (0, 0), (1, 0), (2, -1), (2, 0), (3, -1), (0, 1), (1, 1), (0, 2), (1, 2),
+    (0, 3), (1, 3), (0, 4), (2, 1), (3, 0), (1, 4), (2, 2), (0, 5), (1, 5), (4, 0), (2, 3), (0, 6),
+    (1, 6), (3, 2), (5, 0), (3, 1), (2, 4), (2, 5), (3, 3), (2, 6), (4, 2), (0, 7), (1, 7), (6, 0),
+    (4, 1), (2, 7), (3, 5), (7, 0), (4, 3), (5, 1), (3, 4), (5, 2), (3, 6), (3, 7), (4, 5), (5, 3),
+    (8, 0), (4, 4), (6, 1), (6, 2), (4, 6), (9, 0), (10, 0), (4, 7), (5, 5), (6, 3), (5, 4), (7, 1),
+    (7, 2), (5, 6), (5, 7), (6, 5), (7, 3), (6, 4), (8, 1), (6, 6), (8, 2), (7, 5), (6, 7), (8, 3),
+    (9, 1), (10, 1), (9, 2), (10, 2), (9, 3), (10, 3), (7, 4), (7, 6), (7, 7), (8, 5), (8, 6),
+    (8, 4), (8, 7), (9, 5), (9, 6), (10, 5), (10, 6), (9, 4), (9, 7), (4, -1), (10, 4), (10, 7),
 )
 NT = (((1,), (1,)), ((), ()))
 
@@ -518,7 +516,7 @@
         out_shape=(
             pltpu.VMEM((3, wide, 256), BF16),
             pltpu.VMEM((2, 256, depth), BF16),
-            jax.ShapeDtypeStruct((32, depth), F32),
+            pltpu.VMEM((32, depth), F32),
         ),
         in_specs=[hbm, hbm, vmem, hbm, hbm, hbm],
         out_specs=(hbm, hbm, vmem),
@@ -559,7 +557,7 @@
 GRAD_ROWS = 336
 
 
-def grads_kernel(r, ab, gate_grad, up_grad, down_grad, out, osem):
+def grads_kernel(r, ab, ig, gate_grad, up_grad, down_grad, ig_out, out, osem):
     step = GRAD_ROWS
     n = gate_grad.shape[0] // step
 
@@ -567,6 +565,9 @@
         rows = pl.ds(pl.multiple_of(i * step, 16), step)
         to = (gate_grad, up_grad, down_grad)[part]
         return pltpu.make_async_copy(out.at[part, rows], to.at[rows], osem.at[3 * i + part])
+
+    whole = pltpu.make_async_copy(ig, ig_out, osem.at[3 * n])
+    whole.start()
 
     @pl.loop(0, n)
     def _(i):
@@ -580,9 +581,10 @@
     for i in range(n):
         for part in range(3):
             store(i, part).wait()
-
-
-def grads(r, ab, width):
+    whole.wait()
+
+
+def grads(r, ab, ig, width):
     depth = ab.shape[2]
     assert width % GRAD_ROWS == 0
     n = width // GRAD_ROWS
@@ -590,16 +592,16 @@
     vmem = pl.BlockSpec(memory_space=pltpu.VMEM)
     return pl.pallas_call(
         grads_kernel,
-        in_specs=[vmem, vmem],
-        out_specs=(hbm, hbm, hbm),
-        out_shape=(pltpu.HBM((width, depth), BF16),) * 3,
+        in_specs=[vmem, vmem, vmem],
+        out_specs=(hbm,) * 4,
+        out_shape=(pltpu.HBM((width, depth), BF16),) * 3 + (pltpu.HBM(ig.shape, F32),),
         scratch_shapes=[
             pltpu.VMEM((3, width, depth), BF16),
-            pltpu.SemaphoreType.DMA((3 * n,)),
+            pltpu.SemaphoreType.DMA((3 * n + 1,)),
         ],
         compiler_params=pltpu.CompilerParams(vmem_limit_bytes=24 * 1024 * 1024),
         name="grads",
-    )(r, ab)
+    )(r, ab, ig)
 
 
 def body(tokens, out_grad, token_weight, gate_weight, up_weight, down_weight):
@@ -607,7 +609,7 @@
     r, ab, input_grad = exchange(
         tokens, out_grad, token_weight, gate_weight.T, up_weight.T, down_weight
     )
-    gate_grad, up_grad, down_grad = grads(r, ab, width)
+    gate_grad, up_grad, down_grad, input_grad = grads(r, ab, input_grad, width)
     return input_grad, gate_grad.T, up_grad.T, down_grad
 
 

time: 85.2 us -> 83.1 us (0.975)
  Pallas kernels: 83.8 us -> 82.3 us
    pallas_call x1, Pallas kernels: 78 us -> 76.5 us  [exchange(): pl.pallas_call(functools.partial(exchange_kernel, width), out_shape=(pltp...]
where the time goes in v10:
time: 83.1 us; the launch traced here: 82.9 us
  Pallas kernels  82.3 us (99%)
    pallas_call x1, Pallas kernels, exchange(): pl.pallas_call(functools.partial(exchange_kernel, width), out_shape=(pltp...  76.5 us
    pallas_call x1, Pallas kernels, grads(): pl.pallas_call(grads_kernel, in_specs=[vmem, vmem, vmem], out_specs=(hbm,...  5.85 us

profile of v10, /device:TPU:1, one launch (start us, length us, event | category | flops | bytes accessed | tf_op | source)
XLA Modules:
  0.0 82.9 jit_solution(14361818136773887242)
XLA Ops:
  0.6 76.5 %exchange.1 = (bf16[3,3712,256]{2,1,0:T(8,128)(2,1)S(1)}, bf16[2,256,512]{2,1,0:T(8,128)(2,1)S(1)}, f32[32,512]{1,0:T(8,128)S(1)}) custom-call(bf16[32,512]{1,0:T(8,128)(2,1)} %tok.1, bf16[32,512]{1,0:T(8,128)(2,1)} %og.1, f32[1,256]{1,0:T(1,128)} %bitcast.9, bf16[3696,512]{1,0:T(8,128)(2,1)} %bitcast.5, bf16[3696,512]{1,0:T(8,128)(2,1)} %bitcast.6, ...), custom_call_target="tpu_custom_call" | custom-call | flops 4844421120 | bytes 17031168 | tf_op jit(solution)/shard_map/exchange/pallas_call | solution.py:514
  77.1 5.9 %grads.1 = (bf16[3696,512]{1,0:T(8,128)(2,1)}, bf16[3696,512]{1,0:T(8,128)(2,1)}, bf16[3696,512]{1,0:T(8,128)(2,1)}, f32[32,512]{1,0:T(8,128)}) custom-call(bf16[3,3712,256]{2,1,0:T(8,128)(2,1)S(1)} %get-tuple-element.11.r, bf16[2,256,512]{2,1,0:T(8,128)(2,1)S(1)} %get-tuple-element.12.ab, f32[32,512]{1,0:T(8,128)S(1)} %get-tuple-element.13.ig), custom_call_target="tpu_custom_call" | custom-call | tf_op jit(solution)/shard_map/grads/pallas_call | solution.py:593

commit v11 on v10

--- a/solution.py
+++ b/solution.py
@@ -11,24 +11,24 @@
 MESH = pl.DeviceIdType.MESH
 LANE = 128
 JOBS = (
-    ("E", 4, "xz", "zx"),
-    ("L", 4, "xz", "xz"),
+    ("E", 5, "zx", "xz"),
+    ("L", 5, "zx", "xz"),
     ("T", 5, "zx", "zx"),
-    ("T", 3, "xz", "xz"),
-    ("T", 5, "xz", "xz"),
+    ("T", 2, "xz", "xz"),
     ("T", 5, "zx", "zx"),
-    ("T", 1, "zx", "zx"),
-    ("T", 2, "zx", "xz"),
+    ("T", 4, "xz", "xz"),
+    ("T", 2, "xz", "xz"),
+    ("T", 1, "xz", "xz"),
 )
 ORDER = (
-    (0, -1), (1, -1), (0, 0), (1, 0), (2, -1), (2, 0), (3, -1), (0, 1), (1, 1), (0, 2), (1, 2),
-    (0, 3), (1, 3), (0, 4), (2, 1), (3, 0), (1, 4), (2, 2), (0, 5), (1, 5), (4, 0), (2, 3), (0, 6),
-    (1, 6), (3, 2), (5, 0), (3, 1), (2, 4), (2, 5), (3, 3), (2, 6), (4, 2), (0, 7), (1, 7), (6, 0),
-    (4, 1), (2, 7), (3, 5), (7, 0), (4, 3), (5, 1), (3, 4), (5, 2), (3, 6), (3, 7), (4, 5), (5, 3),
-    (8, 0), (4, 4), (6, 1), (6, 2), (4, 6), (9, 0), (10, 0), (4, 7), (5, 5), (6, 3), (5, 4), (7, 1),
-    (7, 2), (5, 6), (5, 7), (6, 5), (7, 3), (6, 4), (8, 1), (6, 6), (8, 2), (7, 5), (6, 7), (8, 3),
-    (9, 1), (10, 1), (9, 2), (10, 2), (9, 3), (10, 3), (7, 4), (7, 6), (7, 7), (8, 5), (8, 6),
-    (8, 4), (8, 7), (9, 5), (9, 6), (10, 5), (10, 6), (9, 4), (9, 7), (4, -1), (10, 4), (10, 7),
+    (0, -1), (1, -1), (0, 0), (1, 0), (2, -1), (2, 0), (3, -1), (0, 1), (1, 1), (3, 0), (0, 2),
+    (2, 1), (1, 2), (0, 3), (1, 3), (0, 4), (1, 4), (2, 2), (4, 0), (0, 5), (3, 1), (2, 3), (1, 5),
+    (3, 2), (5, 0), (2, 4), (2, 5), (4, 1), (3, 3), (0, 6), (6, 0), (1, 6), (0, 7), (1, 7), (4, 2),
+    (3, 4), (4, 3), (2, 6), (3, 5), (2, 7), (7, 0), (5, 1), (5, 2), (4, 4), (5, 3), (4, 5), (3, 6),
+    (3, 7), (8, 0), (6, 1), (6, 2), (9, 0), (5, 5), (4, 6), (4, 7), (5, 4), (6, 3), (7, 1), (7, 2),
+    (10, 0), (5, 6), (5, 7), (6, 5), (6, 4), (7, 3), (8, 1), (8, 2), (6, 6), (6, 7), (9, 1), (7, 5),
+    (7, 4), (9, 2), (8, 3), (10, 1), (10, 2), (7, 6), (7, 7), (9, 3), (8, 4), (10, 3), (8, 5),
+    (8, 6), (8, 7), (9, 4), (9, 5), (9, 6), (9, 7), (4, -1), (10, 4), (10, 5), (10, 6), (10, 7),
 )
 NT = (((1,), (1,)), ((), ()))
 

time: 83.1 us -> 82.4 us (level)
  no operation moved by 1% of the time
where the time goes in v11:
time: 82.4 us; the launch traced here: 82.3 us
  Pallas kernels  81.7 us (99%)
    pallas_call x1, Pallas kernels, exchange(): pl.pallas_call(functools.partial(exchange_kernel, width), out_shape=(pltp...  75.8 us
    pallas_call x1, Pallas kernels, grads(): pl.pallas_call(grads_kernel, in_specs=[vmem, vmem, vmem], out_specs=(hbm,...  5.85 us

profile of v11, /device:TPU:1, one launch (start us, length us, event | category | flops | bytes accessed | tf_op | source)
XLA Modules:
  0.0 82.3 jit_solution(1487337661148079100)
XLA Ops:
  0.6 75.8 %exchange.1 = (bf16[3,3712,256]{2,1,0:T(8,128)(2,1)S(1)}, bf16[2,256,512]{2,1,0:T(8,128)(2,1)S(1)}, f32[32,512]{1,0:T(8,128)S(1)}) custom-call(bf16[32,512]{1,0:T(8,128)(2,1)} %tok.1, bf16[32,512]{1,0:T(8,128)(2,1)} %og.1, f32[1,256]{1,0:T(1,128)} %bitcast.9, bf16[3696,512]{1,0:T(8,128)(2,1)} %bitcast.5, bf16[3696,512]{1,0:T(8,128)(2,1)} %bitcast.6, ...), custom_call_target="tpu_custom_call" | custom-call | flops 4844421120 | bytes 17031168 | tf_op jit(solution)/shard_map/exchange/pallas_call | solution.py:514
  76.5 5.9 %grads.1 = (bf16[3696,512]{1,0:T(8,128)(2,1)}, bf16[3696,512]{1,0:T(8,128)(2,1)}, bf16[3696,512]{1,0:T(8,128)(2,1)}, f32[32,512]{1,0:T(8,128)}) custom-call(bf16[3,3712,256]{2,1,0:T(8,128)(2,1)S(1)} %get-tuple-element.11.r, bf16[2,256,512]{2,1,0:T(8,128)(2,1)S(1)} %get-tuple-element.12.ab, f32[32,512]{1,0:T(8,128)S(1)} %get-tuple-element.13.ig), custom_call_target="tpu_custom_call" | custom-call | tf_op jit(solution)/shard_map/grads/pallas_call | solution.py:593
